TPU v7x, 32 devices: a whole 2x2x4 slice. The times are simulated.
32 devices in a mesh: sec: 4 (over x, core), tile: 8 (over z, y).
Axes of the slice: x: 2, y: 2, z: 4, core: 2. Of those that a mesh axis runs over, the one named last changes fastest.
Arguments:
- state: float32 [4, 128, 4096], P('sec', None, 'tile'), may hold values from -6 to 6
- tendency: bfloat16 [4, 128, 4096], P('sec', None, 'tile'), may hold values from -4 to 4
- diffusion: bfloat16 [4, 128, 4096], P('sec', None, 'tile'), may hold values from 0.019897461 to 0.23925781
- mixing: float32 [4, 128, 128], P('sec')
- coupling: float32 [4, 128], P('sec'), may hold values from 0.05 to 0.4
- remap_index: int32 [4, 4, 4096], P('sec', None, 'tile'), may hold values from 0 to 1535, as said below
- remap_weight: float32 [4, 4, 4096], P('sec', None, 'tile'), may hold values from 0.1 to 0.4
- active_cols: int32 [4], replicated, may hold values from 256 to 512
- send_cols: int32 [2, 4, 8, 8, 4], P(None, 'sec', 'tile'), may hold values from 0 to 511
- occ_slot: int32 [2, 4, 8, 512], P(None, 'sec', None, 'tile'), may hold values from 0 to 31
- occ_weight: float32 [2, 4, 8, 512], P(None, 'sec', None, 'tile'), may hold values from 0.2 to 0.6
- occ_count: int32 [2, 4, 512], P(None, 'sec', 'tile'), may hold values from 1 to 8
- refraction: float32 [4, 128, 128], P('sec'), may hold values from -0.5 to 0.5
- abel_matrix: float32 [128, 256], replicated
- observed: float32 [2, 512, 256], P(None, ('sec', 'tile')), may hold values from -6 to 6
Outputs:
- final_state: float32 [4, 128, 4096], P('sec', None, 'tile')
- departures: float32 [2, 512, 256], P(None, ('sec', 'tile'))
Inputs may be any that keep to these rules, and one draw needn't show every extreme that they name: `remap_index`: for an atmosphere section the value is a column within the tile of the ocean section; for the last section, value // 512 is the atmosphere section and value % 512 the column within the tile.
All inputs are finite; a program needn't handle non-finite values.
Results may differ from a plain program's by a relative error of at most 0.00035.
Values sent between devices are 32-bit elements; how exact they have to be, the bound alone decides.
A program may use at most 64 MiB of HBM per device.

v0:
```python
import jax
import jax.numpy as jnp
from jax import lax
from jax.sharding import PartitionSpec as P

SUBS = 4
STEPS = 2


def extended(block, sides, width):
    for axis, dim in sides:
        count = lax.axis_size(axis)
        forward = [(i, i + 1) for i in range(count - 1)]
        forward.append((count - 1, 0))
        backward = [(target, source) for source, target in forward]
        low = lax.ppermute(
            lax.slice_in_dim(block, block.shape[dim] - width, None, axis=dim), axis, forward
        )
        high = lax.ppermute(lax.slice_in_dim(block, 0, width, axis=dim), axis, backward)
        block = jnp.concatenate([low, block, high], axis=dim)
    return block


def observe(arrived_rows, slots, weights, counts, refraction, abel_matrix, observed_step):
    highest = lax.Precision.HIGHEST
    gathered = jnp.take(arrived_rows, slots, axis=0)
    tangent_rank = jnp.arange(slots.shape[0], dtype=jnp.int32)[:, None]
    live_weight = jnp.where(tangent_rank < counts[None, :], weights, 0.0)
    profile = jnp.sum(live_weight[:, :, None] * gathered, axis=0)
    projected = jnp.dot(profile, refraction, precision=highest, preferred_element_type=jnp.float32)
    bending = jnp.dot(projected, abel_matrix, precision=highest, preferred_element_type=jnp.float32)
    owned = lax.psum_scatter(bending, "sec", scatter_dimension=0, tiled=True)
    return observed_step - owned


def shards(
    state,
    tendency,
    diffusion,
    mixing,
    coupling,
    remap_index,
    remap_weight,
    active_cols,
    send_cols,
    occ_slot,
    occ_weight,
    occ_count,
    refraction,
    abel_matrix,
    observed,
):
    highest = lax.Precision.HIGHEST
    section = lax.axis_index("sec")
    sections = lax.axis_size("sec")
    tile_count = lax.axis_size("tile")
    levels = state.shape[1]
    columns = state.shape[2]
    field = state[0]
    live_limit = lax.dynamic_index_in_dim(active_cols, section, 0, keepdims=False)
    live_mask = jnp.arange(columns, dtype=jnp.int32) < live_limit
    is_ocean = section == sections - 1
    position = jnp.where(is_ocean, remap_index[0], (sections - 1) * columns + remap_index[0])
    rates = diffusion[0]
    forcing = tendency[0].astype(jnp.float32)
    matrix = mixing[0]
    response = coupling[0][:, None]
    outgoing = []
    finished = []
    for period in range(STEPS):
        surface = field[levels - 1]
        surfaces = lax.all_gather(surface[None], "sec", axis=0, tiled=True)
        picked = jnp.take(surfaces.reshape(-1), position)
        boundary = jnp.sum(remap_weight[0] * picked, axis=0) - surface
        for substep in range(SUBS):
            padded = extended(field, (("tile", 1),), 1)
            spread = field + rates * (padded[:, :-2] + padded[:, 2:] - 2.0 * field)
            stepped = jnp.dot(matrix, spread, precision=highest, preferred_element_type=jnp.float32)
            stepped = stepped + response * boundary[None, :] + forcing
            field = jnp.where(live_mask[None, :], stepped, field)
        chosen = jnp.take(field, send_cols[period, 0, 0].reshape(-1), axis=1)
        parcel = chosen.T.reshape(tile_count, -1, levels)
        outgoing.append(parcel)
    arrived = lax.all_to_all(
        jnp.stack(outgoing, 1), "tile", split_axis=0, concat_axis=0, tiled=True
    )
    for period in range(STEPS):
        finished.append(
            observe(
                arrived[:, period].reshape(-1, levels),
                occ_slot[period, 0],
                occ_weight[period, 0],
                occ_count[period, 0],
                refraction[0],
                abel_matrix,
                observed[period],
            )
        )
    return (field[None], jnp.stack(finished))


def solution(mesh):
    return jax.shard_map(
        shards,
        mesh=mesh,
        in_specs=(
            P("sec", None, "tile"),
            P("sec", None, "tile"),
            P("sec", None, "tile"),
            P("sec", None, None),
            P("sec", None),
            P("sec", None, "tile"),
            P("sec", None, "tile"),
            P(),
            P(None, "sec", "tile", None, None),
            P(None, "sec", None, "tile"),
            P(None, "sec", None, "tile"),
            P(None, "sec", "tile"),
            P("sec", None, None),
            P(),
            P(None, ("sec", "tile"), None),
        ),
        out_specs=(P("sec", None, "tile"), P(None, ("sec", "tile"), None)),
        check_vma=False,
    )
```

profile of v0, /device:TPU:0, one launch (start us, length us, event | category | flops | bytes accessed | tf_op | source)
XLA Modules:
  0.0 168.1 jit_solution(16455860285563002752)
XLA Ops:
  7.2 1.1 copy.30
  8.3 3.0 %collective-permute-start = (f32[128,1]{0,1:T(1,128)S(1)}, f32[128,1]{0,1:T(1,128)S(1)}, u32[]{:S(2)}, u32[]{:S(2)}) collective-permute-start(f32[128,1]{0,1:T(1,128)S(1)} %get-tuple-element.25), channel_id=1, source_target_pairs={{0,1},{1,2},{2,3},{3,4},{4,5},{5,6},{6,7},{7,0},{8,9},{9,10},{10,1... | collective-permute-start | bytes 1544 | tf_op jit(solution)/shard_map/ppermute | solution.py:16
  11.3 3.1 %collective-permute-start.1 = (f32[128,1]{0,1:T(1,128)S(1)}, f32[128,1]{0,1:T(1,128)S(1)}, u32[]{:S(2)}, u32[]{:S(2)}) collective-permute-start(f32[128,1]{0,1:T(1,128)S(1)} %get-tuple-element.26), channel_id=1, source_target_pairs={{1,0},{2,1},{3,2},{4,3},{5,4},{6,5},{7,6},{0,7},{9,8},{10,9},{11,1... | collective-permute-start | bytes 1544 | tf_op jit(solution)/shard_map/ppermute | solution.py:19
  14.4 0.7 slice.163
  15.4 0.5 copy-done.6
  15.9 0.7 copy-done.10
  16.6 5.1 %all-gather = f32[4,1,512]{2,1,0:T(1,128)S(1)} all-gather(f32[1,1,512]{2,1,0:T(1,128)S(1)} %slice.163), channel_id=2, replica_groups=mesh['sec'=4,'tile'=8] {'sec'}, dimensions={0}, use_global_device_ids=true | all-gather | bytes 10240 | tf_op jit(solution)/shard_map/all_gather | solution.py:72
  21.8 11.8 %gather_fusion = f32[2048]{0:T(1024)S(1)} fusion(f32[2048]{0:T(1024)S(1)} %bitcast.213, s32[2048]{0:T(1024)S(1)} %broadcast_clamp_fusion), kind=kCustom, calls=%fused_computation.clone | custom fusion | bytes 24576 | tf_op jit(solution)/shard_map/jit(_take)/gather | solution.py:73
  33.6 0.6 copy-done.12
  34.3 0.6 dynamic_slice.4
  34.9 0.7 iota_compare_fusion.2
  35.8 0.8 copy-done.3
  36.8 0.7 copy-done.11
  37.5 0.4 fusion.23
  38.0 4.7 %collective-permute-start.3 = (f32[128,1]{0,1:T(1,128)S(1)}, f32[128,1]{0,1:T(1,128)S(1)}, u32[]{:S(2)}, u32[]{:S(2)}) collective-permute-start(f32[128,1]{0,1:T(1,128)S(1)} %get-tuple-element.24), channel_id=1, source_target_pairs={{1,0},{2,1},{3,2},{4,3},{5,4},{6,5},{7,6},{0,7},{9,8},{10,9},{11,1... | collective-permute-start | bytes 1544 | tf_op jit(solution)/shard_map/ppermute | solution.py:19
  42.7 1.5 collective-permute-done.2
  44.2 0.4 fusion.20
  44.7 4.8 %collective-permute-start.5 = (f32[128,1]{0,1:T(1,128)S(1)}, f32[128,1]{0,1:T(1,128)S(1)}, u32[]{:S(2)}, u32[]{:S(2)}) collective-permute-start(f32[128,1]{0,1:T(1,128)S(1)} %get-tuple-element.22), channel_id=1, source_target_pairs={{1,0},{2,1},{3,2},{4,3},{5,4},{6,5},{7,6},{0,7},{9,8},{10,9},{11,1... | collective-permute-start | bytes 1544 | tf_op jit(solution)/shard_map/ppermute | solution.py:19
  49.5 1.4 collective-permute-done.4
  51.0 0.4 fusion.17
  51.5 4.8 %collective-permute-start.7 = (f32[128,1]{0,1:T(1,128)S(1)}, f32[128,1]{0,1:T(1,128)S(1)}, u32[]{:S(2)}, u32[]{:S(2)}) collective-permute-start(f32[128,1]{0,1:T(1,128)S(1)} %get-tuple-element.20), channel_id=1, source_target_pairs={{1,0},{2,1},{3,2},{4,3},{5,4},{6,5},{7,6},{0,7},{9,8},{10,9},{11,1... | collective-permute-start | bytes 1544 | tf_op jit(solution)/shard_map/ppermute | solution.py:19
  56.3 1.4 collective-permute-done.6
  58.5 5.2 %all-gather.1 = f32[4,1,512]{2,1,0:T(1,128)S(1)} all-gather(f32[1,1,512]{2,1,0:T(1,128)S(1)} %bitcast.226), channel_id=1, replica_groups=mesh['sec'=4,'tile'=8] {'sec'}, dimensions={0}, use_global_device_ids=true | all-gather | bytes 10240 | tf_op jit(solution)/shard_map/all_gather | solution.py:72
  63.6 11.8 %gather_fusion.1 = f32[2048]{0:T(1024)S(1)} fusion(f32[2048]{0:T(1024)S(1)} %bitcast.214, s32[2048]{0:T(1024)S(1)} %broadcast_clamp_fusion), kind=kCustom, calls=%fused_computation.3.clone | custom fusion | bytes 24576 | tf_op jit(solution)/shard_map/jit(_take)/gather | solution.py:73
  75.5 4.8 %collective-permute-start.9 = (f32[128,1]{0,1:T(1,128)S(1)}, f32[128,1]{0,1:T(1,128)S(1)}, u32[]{:S(2)}, u32[]{:S(2)}) collective-permute-start(f32[128,1]{0,1:T(1,128)S(1)} %get-tuple-element.18), channel_id=1, source_target_pairs={{1,0},{2,1},{3,2},{4,3},{5,4},{6,5},{7,6},{0,7},{9,8},{10,9},{11,1... | collective-permute-start | bytes 1544 | tf_op jit(solution)/shard_map/ppermute | solution.py:19
  80.8 1.1 collective-permute-done.8
  81.8 0.4 fusion.11
  82.3 4.8 %collective-permute-start.11 = (f32[128,1]{0,1:T(1,128)S(1)}, f32[128,1]{0,1:T(1,128)S(1)}, u32[]{:S(2)}, u32[]{:S(2)}) collective-permute-start(f32[128,1]{0,1:T(1,128)S(1)} %get-tuple-element.16), channel_id=1, source_target_pairs={{1,0},{2,1},{3,2},{4,3},{5,4},{6,5},{7,6},{0,7},{9,8},{10,9},{11,1... | collective-permute-start | bytes 1544 | tf_op jit(solution)/shard_map/ppermute | solution.py:19
  87.3 1.4 collective-permute-done.10
  89.2 4.8 %collective-permute-start.13 = (f32[128,1]{0,1:T(1,128)S(1)}, f32[128,1]{0,1:T(1,128)S(1)}, u32[]{:S(2)}, u32[]{:S(2)}) collective-permute-start(f32[128,1]{0,1:T(1,128)S(1)} %get-tuple-element.14), channel_id=1, source_target_pairs={{1,0},{2,1},{3,2},{4,3},{5,4},{6,5},{7,6},{0,7},{9,8},{10,9},{11,1... | collective-permute-start | bytes 1544 | tf_op jit(solution)/shard_map/ppermute | solution.py:19
  94.1 0.6 gather_fusion.2
  94.6 0.8 collective-permute-done.12
  96.0 4.8 %collective-permute-start.15 = (f32[128,1]{0,1:T(1,128)S(1)}, f32[128,1]{0,1:T(1,128)S(1)}, u32[]{:S(2)}, u32[]{:S(2)}) collective-permute-start(f32[128,1]{0,1:T(1,128)S(1)} %get-tuple-element.12), channel_id=1, source_target_pairs={{1,0},{2,1},{3,2},{4,3},{5,4},{6,5},{7,6},{0,7},{9,8},{10,9},{11,1... | collective-permute-start | bytes 1544 | tf_op jit(solution)/shard_map/ppermute | solution.py:19
  100.9 1.4 collective-permute-done.14
  102.7 0.6 gather_fusion.3
  103.3 0.6 pad_maximum_fusion.24
  104.0 6.1 %all-to-all-start = ((f32[8,2,4,128]{3,2,1,0:T(4,128)}), f32[8,2,4,128]{3,2,1,0:T(4,128)S(1)}, u32[]{:S(2)}, u32[]{:S(2)}) async-start(f32[8,2,4,128]{3,2,1,0:T(4,128)} %pad_maximum_fusion.24), calls=%async_computation | async-start | bytes 65536 | tf_op jit(solution)/shard_map/all_to_all | solution.py:84
  110.1 6.6 %all-to-all-done = f32[8,2,4,128]{3,2,1,0:T(4,128)S(1)} async-done(((f32[8,2,4,128]{3,2,1,0:T(4,128)}), f32[8,2,4,128]{3,2,1,0:T(4,128)S(1)}, u32[]{:S(2)}, u32[]{:S(2)}) %all-to-all-start) | async-done | bytes 32800 | tf_op jit(solution)/shard_map/all_to_all | solution.py:84
  116.7 1.0 gather_fusion.5
  117.8 1.0 gather_fusion.4
  119.2 0.5 copy-done.1
  120.0 0.8 fusion.149
  120.9 0.8 fusion.150
  121.8 0.8 copy.38
  122.6 15.3 %reduce-scatter.3.cloned.1.call-done = f32[16,256]{1,0:T(8,128)} async-done(((f32[64,256]{1,0:T(8,128)}), f32[16,256]{1,0:T(8,128)}) %reduce-scatter.3.cloned.1.call-update) | async-done | bytes 16400 | tf_op jit(solution)/shard_map/reduce_scatter | solution.py:32
  137.9 22.0 %reduce-scatter.5.cloned.1.call-done = f32[16,256]{1,0:T(8,128)} async-done(((f32[64,256]{1,0:T(8,128)}), f32[16,256]{1,0:T(8,128)}) %reduce-scatter.5.cloned.1.call-update) | async-done | bytes 16400 | tf_op jit(solution)/shard_map/reduce_scatter | solution.py:32
  159.9 0.7 fusion.119
  160.7 0.6 pad_maximum_fusion.25
  (92 shorter events, 4.7 us)
Async XLA Ops:
  7.2 112.9 %copy-start = (f32[128,256]{1,0:T(8,128)S(1)}, f32[128,256]{1,0:T(8,128)}, u32[]{:S(2)}) copy-start(f32[128,256]{1,0:T(8,128)} %param.34) | copy-start | bytes 393220
  8.3 6.9 %copy-start.9 = (s32[2,1,1,8,4]{3,4,2,1,0:T(4,128)S(1)}, s32[2,1,1,8,4]{3,4,2,1,0:T(4,128)}, u32[]{:S(2)}) copy-start(s32[2,1,1,8,4]{3,4,2,1,0:T(4,128)} %param.29) | copy-start | bytes 772
  8.3 28.4 %collective-permute-start = (f32[128,1]{0,1:T(1,128)S(1)}, f32[128,1]{0,1:T(1,128)S(1)}, u32[]{:S(2)}, u32[]{:S(2)}) collective-permute-start(f32[128,1]{0,1:T(1,128)S(1)} %get-tuple-element.25), channel_id=1, source_target_pairs={{0,1},{1,2},{2,3},{3,4},{4,5},{5,6},{6,7},{7,0},{8,9},{9,10},{10,1... | collective-permute-start | bytes 1544 | tf_op jit(solution)/shard_map/ppermute | solution.py:16
  11.3 25.4 %collective-permute-start.1 = (f32[128,1]{0,1:T(1,128)S(1)}, f32[128,1]{0,1:T(1,128)S(1)}, u32[]{:S(2)}, u32[]{:S(2)}) collective-permute-start(f32[128,1]{0,1:T(1,128)S(1)} %get-tuple-element.26), channel_id=1, source_target_pairs={{1,0},{2,1},{3,2},{4,3},{5,4},{6,5},{7,6},{0,7},{9,8},{10,9},{11,1... | collective-permute-start | bytes 1544 | tf_op jit(solution)/shard_map/ppermute | solution.py:19
  15.2 0.7 copy-start.6
  15.9 0.7 copy-start.10
  15.9 5.8 %copy-start.4 = (s32[1,4,512]{2,1,0:T(4,128)S(1)}, s32[1,4,512]{2,1,0:T(4,128)}, u32[]{:S(2)}) copy-start(s32[1,4,512]{2,1,0:T(4,128)} %param.26) | copy-start | bytes 24580
  21.8 13.1 %copy-start.8 = (f32[2,1,8,64]{3,2,1,0:T(8,128)S(1)}, f32[2,1,8,64]{3,2,1,0:T(8,128)}, u32[]{:S(2)}) copy-start(f32[2,1,8,64]{3,2,1,0:T(8,128)} %param.31) | copy-start | bytes 12292
  21.8 13.9 %copy-start.2 = (bf16[1,128,512]{2,1,0:T(8,128)(2,1)S(1)}, bf16[1,128,512]{2,1,0:T(8,128)(2,1)}, u32[]{:S(2)}) copy-start(bf16[1,128,512]{2,1,0:T(8,128)(2,1)} %param.22) | copy-start | bytes 393220
  33.6 1.3 copy-start.7
  33.6 0.7 copy-start.12
  35.7 0.9 copy-start.3
  36.6 0.8 copy-start.11
  36.8 0.7 copy-start.13
  37.9 6.3 %collective-permute-start.2 = (f32[128,1]{0,1:T(1,128)S(1)}, f32[128,1]{0,1:T(1,128)S(1)}, u32[]{:S(2)}, u32[]{:S(2)}) collective-permute-start(f32[128,1]{0,1:T(1,128)S(1)} %get-tuple-element.23), channel_id=1, source_target_pairs={{0,1},{1,2},{2,3},{3,4},{4,5},{5,6},{6,7},{7,0},{8,9},{9,10},{10,1... | collective-permute-start | bytes 1544 | tf_op jit(solution)/shard_map/ppermute | solution.py:16
  38.0 6.2 %collective-permute-start.3 = (f32[128,1]{0,1:T(1,128)S(1)}, f32[128,1]{0,1:T(1,128)S(1)}, u32[]{:S(2)}, u32[]{:S(2)}) collective-permute-start(f32[128,1]{0,1:T(1,128)S(1)} %get-tuple-element.24), channel_id=1, source_target_pairs={{1,0},{2,1},{3,2},{4,3},{5,4},{6,5},{7,6},{0,7},{9,8},{10,9},{11,1... | collective-permute-start | bytes 1544 | tf_op jit(solution)/shard_map/ppermute | solution.py:19
  44.7 6.3 %collective-permute-start.4 = (f32[128,1]{0,1:T(1,128)S(1)}, f32[128,1]{0,1:T(1,128)S(1)}, u32[]{:S(2)}, u32[]{:S(2)}) collective-permute-start(f32[128,1]{0,1:T(1,128)S(1)} %get-tuple-element.21), channel_id=1, source_target_pairs={{0,1},{1,2},{2,3},{3,4},{4,5},{5,6},{6,7},{7,0},{8,9},{9,10},{10,1... | collective-permute-start | bytes 1544 | tf_op jit(solution)/shard_map/ppermute | solution.py:16
  44.7 6.2 %collective-permute-start.5 = (f32[128,1]{0,1:T(1,128)S(1)}, f32[128,1]{0,1:T(1,128)S(1)}, u32[]{:S(2)}, u32[]{:S(2)}) collective-permute-start(f32[128,1]{0,1:T(1,128)S(1)} %get-tuple-element.22), channel_id=1, source_target_pairs={{1,0},{2,1},{3,2},{4,3},{5,4},{6,5},{7,6},{0,7},{9,8},{10,9},{11,1... | collective-permute-start | bytes 1544 | tf_op jit(solution)/shard_map/ppermute | solution.py:19
  51.4 6.4 %collective-permute-start.6 = (f32[128,1]{0,1:T(1,128)S(1)}, f32[128,1]{0,1:T(1,128)S(1)}, u32[]{:S(2)}, u32[]{:S(2)}) collective-permute-start(f32[128,1]{0,1:T(1,128)S(1)} %get-tuple-element.19), channel_id=1, source_target_pairs={{0,1},{1,2},{2,3},{3,4},{4,5},{5,6},{6,7},{7,0},{8,9},{9,10},{10,1... | collective-permute-start | bytes 1544 | tf_op jit(solution)/shard_map/ppermute | solution.py:16
  51.5 6.3 %collective-permute-start.7 = (f32[128,1]{0,1:T(1,128)S(1)}, f32[128,1]{0,1:T(1,128)S(1)}, u32[]{:S(2)}, u32[]{:S(2)}) collective-permute-start(f32[128,1]{0,1:T(1,128)S(1)} %get-tuple-element.20), channel_id=1, source_target_pairs={{1,0},{2,1},{3,2},{4,3},{5,4},{6,5},{7,6},{0,7},{9,8},{10,9},{11,1... | collective-permute-start | bytes 1544 | tf_op jit(solution)/shard_map/ppermute | solution.py:19
  75.5 6.3 %collective-permute-start.8 = (f32[128,1]{0,1:T(1,128)S(1)}, f32[128,1]{0,1:T(1,128)S(1)}, u32[]{:S(2)}, u32[]{:S(2)}) collective-permute-start(f32[128,1]{0,1:T(1,128)S(1)} %get-tuple-element.17), channel_id=1, source_target_pairs={{0,1},{1,2},{2,3},{3,4},{4,5},{5,6},{6,7},{7,0},{8,9},{9,10},{10,1... | collective-permute-start | bytes 1544 | tf_op jit(solution)/shard_map/ppermute | solution.py:16
  75.5 6.3 %collective-permute-start.9 = (f32[128,1]{0,1:T(1,128)S(1)}, f32[128,1]{0,1:T(1,128)S(1)}, u32[]{:S(2)}, u32[]{:S(2)}) collective-permute-start(f32[128,1]{0,1:T(1,128)S(1)} %get-tuple-element.18), channel_id=1, source_target_pairs={{1,0},{2,1},{3,2},{4,3},{5,4},{6,5},{7,6},{0,7},{9,8},{10,9},{11,1... | collective-permute-start | bytes 1544 | tf_op jit(solution)/shard_map/ppermute | solution.py:19
  82.3 6.4 %collective-permute-start.10 = (f32[128,1]{0,1:T(1,128)S(1)}, f32[128,1]{0,1:T(1,128)S(1)}, u32[]{:S(2)}, u32[]{:S(2)}) collective-permute-start(f32[128,1]{0,1:T(1,128)S(1)} %get-tuple-element.15), channel_id=1, source_target_pairs={{0,1},{1,2},{2,3},{3,4},{4,5},{5,6},{6,7},{7,0},{8,9},{9,10},{10,1... | collective-permute-start | bytes 1544 | tf_op jit(solution)/shard_map/ppermute | solution.py:16
  82.3 6.3 %collective-permute-start.11 = (f32[128,1]{0,1:T(1,128)S(1)}, f32[128,1]{0,1:T(1,128)S(1)}, u32[]{:S(2)}, u32[]{:S(2)}) collective-permute-start(f32[128,1]{0,1:T(1,128)S(1)} %get-tuple-element.16), channel_id=1, source_target_pairs={{1,0},{2,1},{3,2},{4,3},{5,4},{6,5},{7,6},{0,7},{9,8},{10,9},{11,1... | collective-permute-start | bytes 1544 | tf_op jit(solution)/shard_map/ppermute | solution.py:19
  89.1 6.4 %collective-permute-start.12 = (f32[128,1]{0,1:T(1,128)S(1)}, f32[128,1]{0,1:T(1,128)S(1)}, u32[]{:S(2)}, u32[]{:S(2)}) collective-permute-start(f32[128,1]{0,1:T(1,128)S(1)} %get-tuple-element.13), channel_id=1, source_target_pairs={{0,1},{1,2},{2,3},{3,4},{4,5},{5,6},{6,7},{7,0},{8,9},{9,10},{10,1... | collective-permute-start | bytes 1544 | tf_op jit(solution)/shard_map/ppermute | solution.py:16
  89.2 6.3 %collective-permute-start.13 = (f32[128,1]{0,1:T(1,128)S(1)}, f32[128,1]{0,1:T(1,128)S(1)}, u32[]{:S(2)}, u32[]{:S(2)}) collective-permute-start(f32[128,1]{0,1:T(1,128)S(1)} %get-tuple-element.14), channel_id=1, source_target_pairs={{1,0},{2,1},{3,2},{4,3},{5,4},{6,5},{7,6},{0,7},{9,8},{10,9},{11,1... | collective-permute-start | bytes 1544 | tf_op jit(solution)/shard_map/ppermute | solution.py:19
  95.9 6.4 %collective-permute-start.14 = (f32[128,1]{0,1:T(1,128)S(1)}, f32[128,1]{0,1:T(1,128)S(1)}, u32[]{:S(2)}, u32[]{:S(2)}) collective-permute-start(f32[128,1]{0,1:T(1,128)S(1)} %get-tuple-element.11), channel_id=1, source_target_pairs={{0,1},{1,2},{2,3},{3,4},{4,5},{5,6},{6,7},{7,0},{8,9},{9,10},{10,1... | collective-permute-start | bytes 1544 | tf_op jit(solution)/shard_map/ppermute | solution.py:16
  96.0 6.3 %collective-permute-start.15 = (f32[128,1]{0,1:T(1,128)S(1)}, f32[128,1]{0,1:T(1,128)S(1)}, u32[]{:S(2)}, u32[]{:S(2)}) collective-permute-start(f32[128,1]{0,1:T(1,128)S(1)} %get-tuple-element.12), channel_id=1, source_target_pairs={{1,0},{2,1},{3,2},{4,3},{5,4},{6,5},{7,6},{0,7},{9,8},{10,9},{11,1... | collective-permute-start | bytes 1544 | tf_op jit(solution)/shard_map/ppermute | solution.py:19
  104.0 12.7 %all-to-all-start = ((f32[8,2,4,128]{3,2,1,0:T(4,128)}), f32[8,2,4,128]{3,2,1,0:T(4,128)S(1)}, u32[]{:S(2)}, u32[]{:S(2)}) async-start(f32[8,2,4,128]{3,2,1,0:T(4,128)} %pad_maximum_fusion.24), calls=%async_computation | async-start | bytes 65536 | tf_op jit(solution)/shard_map/all_to_all | solution.py:84
  110.0 27.9 %reduce-scatter.3.cloned.1.call-start = ((), (), s32[]{:S(2)}) async-start(), calls=%async_computation.3 | async-start | bytes 81920 | tf_op jit(solution)/shard_map/reduce_scatter | solution.py:32
  118.8 0.8 copy-start.1
  120.9 39.1 %reduce-scatter.5.cloned.1.call-start = ((), (), s32[]{:S(2)}) async-start(), calls=%async_computation.4 | async-start | bytes 81920 | tf_op jit(solution)/shard_map/reduce_scatter | solution.py:32
  121.8 38.2 %copy-start.5 = (f32[2,16,256]{2,1,0:T(8,128)S(1)}, f32[2,16,256]{2,1,0:T(8,128)}, u32[]{:S(2)}) copy-start(f32[2,16,256]{2,1,0:T(8,128)} %param.35) | copy-start | bytes 98308
Sparse Core Ops, SparseCore 0:
  121.0 16.8 reduce-scatter.2
  140.5 19.4 reduce-scatter.4
where the time goes:
time: 169 us; the launch traced here: 168 us
  waiting for transfers between devices  53 us (31%)
  starting transfers between devices  46.3 us (27%)
  local copies, waits for them, and re-layouts  35 us (21%)
  between operations  14.5 us (9%)
  blocking collectives  10.3 us (6%)
  matrix products  5.53 us (3%)
  other arithmetic  3.5 us (2%)
    reduce_scatter x2, waiting for transfers between devices, observe(): owned = lax.psum_scatter(bending, 'sec', scatter_dimension=0, tiled=True)  37.3 us
    ppermute x8, starting transfers between devices, extended(): lax.ppermute(lax.slice_in_dim(block, 0, width, axis=dim), axis, backward)  36.7 us
    gather x4, local copies, waits for them, and re-layouts, shards(): picked = jnp.take(surfaces.reshape(-1), position)  23.6 us
    all_gather x2, blocking collectives, shards(): surfaces = lax.all_gather(surface[None], 'sec', axis=0, tiled=True)  10.3 us
    ppermute x8, waiting for transfers between devices, extended(): lax.ppermute(lax.slice_in_dim(block, block.shape[dim] - width, None, axis...  9.02 us
    all_to_all x1, waiting for transfers between devices, shards(): lax.all_to_all(jnp.stack(outgoing, 1), 'tile', split_axis=0, concat_axis=...  6.63 us
    all_to_all x1, starting transfers between devices, shards(): lax.all_to_all(jnp.stack(outgoing, 1), 'tile', split_axis=0, concat_axis=...  6.06 us
    unnamed x33, local copies, waits for them, and re-layouts  5.99 us
  transfers between devices with their start and end apart: 19, of which 10 were waited for; matrix products, arithmetic and copies ran while one was open for 10% of the time, Pallas kernels for 0%

commit v1 on v0

v1 whole, which is shorter than its diff:
```python
import functools

import jax
import jax.numpy as jnp
from jax import lax
from jax.experimental import pallas as pl
from jax.experimental.pallas import tpu as pltpu
from jax.sharding import PartitionSpec as P

SUBS = 4
STEPS = 2
HALO = SUBS * STEPS
LANES = 128
PACK = 3 * HALO + 8
F32 = jnp.float32
BF16 = jnp.bfloat16
MESH = pl.DeviceIdType.MESH


def split(x):
    high = x.astype(BF16)
    low = (x - high.astype(F32)).astype(BF16)
    return high, low


def mm(a, b, dims):
    return lax.dot_general(a, b, (dims, ((), ())), preferred_element_type=F32)


NN = ((1,), (0,))
NT = ((1,), (1,))
TN = ((0,), (0,))


def dot3(a, b, dims=NN):
    ah, al = split(a)
    bh, bl = split(b)
    return mm(ah, bh, dims) + (mm(ah, bl, dims) + mm(al, bh, dims))


def kernel(
    sections,
    tiles,
    state,
    tendency,
    diffusion,
    mixing,
    coupling,
    remap_index,
    remap_weight,
    active_cols,
    send_cols,
    occ_slot,
    occ_weight,
    occ_count,
    refraction,
    abel_matrix,
    observed,
    out_state,
    out_departures,
    field,
    rates,
    forcing,
    tend_v,
    diff_v,
    mix_v,
    coup_v,
    ridx_v,
    rw_v,
    cols_v,
    slot_v,
    ow_v,
    oc_v,
    refr_v,
    abel_v,
    obs_v,
    dep_v,
    mix_a,
    mix_b,
    gain,
    position,
    weight,
    picked,
    surf,
    tab,
    pack_out,
    pack_in,
    chosen_out,
    chosen_in,
    parts_out,
    parts_in,
    load_sem,
    store_sem,
    pack_send,
    pack_recv,
    surf_send,
    surf_recv,
    col_send,
    col_recv,
    red_send,
    red_recv,
):
    levels, columns = tend_v.shape
    ext = field.shape[1]
    blocks = columns // LANES
    rk = ridx_v.shape[0]
    s = lax.axis_index("sec")
    t = lax.axis_index("tile")
    ocean = sections - 1
    is_ocean = s == ocean
    right = lax.rem(t + 1, tiles)
    left = lax.rem(t + tiles - 1, tiles)
    near = ((t, 0), (left, 1), (right, 2))

    loads = [
        (state.at[0], field.at[:, 0:columns]),
        (diffusion.at[0], diff_v),
        (tendency.at[0], tend_v),
        (remap_index.at[0], ridx_v),
        (remap_weight.at[0], rw_v),
        (mixing.at[0], mix_v),
        (coupling, coup_v),
        (send_cols, cols_v),
        (occ_slot, slot_v),
        (occ_weight, ow_v),
        (occ_count, oc_v),
        (refraction.at[0], refr_v),
        (abel_matrix, abel_v),
        (observed, obs_v),
    ]
    loads = [pltpu.make_async_copy(a, b, load_sem.at[i]) for i, (a, b) in enumerate(loads)]
    for load in loads:
        load.start()

    def over_tiles(body):
        if tiles <= 8:
            for d in range(1, tiles):
                body(lax.rem(t + d, tiles))
        else:
            lax.fori_loop(1, tiles, lambda d, c: (body(lax.rem(t + d, tiles)), c)[1], 0)

    barrier = pltpu.get_barrier_semaphore()

    def greet(sec, tile):
        pl.semaphore_signal(barrier, inc=1, device_id=(sec, tile), device_id_type=MESH)

    over_tiles(lambda other: greet(s, other))
    for d in range(1, sections):
        greet(lax.rem(s + d, sections), t)

    @pl.when(is_ocean)
    def _():
        for a in range(ocean):
            greet(a, left)
            greet(a, right)

    @pl.when(jnp.logical_not(is_ocean))
    def _():
        greet(ocean, left)
        greet(ocean, right)

    lane = lax.broadcasted_iota(jnp.int32, (levels, LANES), 1)
    row_lane = lax.broadcasted_iota(jnp.int32, (1, LANES), 1)

    for load in loads[:5]:
        load.wait()
    surf[0] = field[levels - 1 : levels, 0:columns]

    tail = columns - LANES
    idx_f = ridx_v[...].astype(F32)

    def pack(slot, lo, shift):
        a = field[:, lo : lo + LANES]
        b = diff_v[:, lo : lo + LANES].astype(F32)
        c = tend_v[:, lo : lo + LANES].astype(F32)
        if shift:
            a = pltpu.roll(a, shift, 1)
        b = pltpu.roll(b, shift + HALO, 1)
        c = pltpu.roll(c, shift + 2 * HALO, 1)
        mixed = jnp.where(lane < HALO, a, jnp.where(lane < 2 * HALO, b, c))
        pack_out[slot, 0 : 3 * HALO, :] = mixed.T[0 : 3 * HALO]
        pack_out[slot, 3 * HALO : 3 * HALO + rk, :] = idx_f[:, lo : lo + LANES]
        pack_out[slot, 3 * HALO + rk : PACK, :] = rw_v[:, lo : lo + LANES]

    pack(0, 0, 0)
    pack(1, tail, HALO)

    meet = (tiles - 1) + (sections - 1) + jnp.where(is_ocean, 2 * ocean, 2)
    pl.semaphore_wait(barrier, meet)

    def pack_copy(slot, tile):
        return pltpu.make_async_remote_copy(
            src_ref=pack_out.at[slot],
            dst_ref=pack_in.at[slot],
            send_sem=pack_send.at[slot],
            recv_sem=pack_recv.at[slot],
            device_id=(s, tile),
            device_id_type=MESH,
        )

    def surf_copy(p, d, a, sec, tile, mark):
        return pltpu.make_async_remote_copy(
            src_ref=surf.at[p],
            dst_ref=tab.at[p, d, a],
            send_sem=surf_send.at[p, d, mark],
            recv_sem=surf_recv.at[p, d, a],
            device_id=(sec, tile),
            device_id_type=MESH,
        )

    def surf_each(p, act):
        @pl.when(is_ocean)
        def _():
            for tile, d in near:
                for a in range(ocean):
                    act(surf_copy(p, d, 0, a, tile, a))

        @pl.when(jnp.logical_not(is_ocean))
        def _():
            for tile, d in near:
                act(surf_copy(p, d, s, ocean, tile, 0))

    packs = (pack_copy(0, left), pack_copy(1, right))
    for copy in packs:
        copy.start()
    surf_each(0, lambda copy: copy.start())

    for load in loads[5:]:
        load.wait()
    mh, ml = split(mix_v[...])
    mix_a[:, 0:levels] = mh
    mix_a[:, levels : 2 * levels] = mh
    mix_b[...] = ml
    gain[...] = jnp.broadcast_to(coup_v[...], (LANES, levels)).T
    rates[:, 0:columns] = diff_v[...].astype(F32)
    forcing[:, 0:columns] = tend_v[...].astype(F32)
    for b in range(blocks):
        position[b * rk : (b + 1) * rk, :] = ridx_v[:, b * LANES : (b + 1) * LANES]
        weight[b * rk : (b + 1) * rk, :] = rw_v[:, b * LANES : (b + 1) * LANES]

    limit = active_cols[s]
    number = lax.broadcasted_iota(jnp.int32, (1, ext), 1)
    number = jnp.where(
        number < columns, number, jnp.where(number < columns + LANES // 2, number - columns, number - LANES)
    )
    live = number < limit

    cap = cols_v.shape[4]
    rows = tiles * 8

    def selector(p):
        which = lax.broadcasted_iota(jnp.int32, (rows, tiles), 0)
        owner = lax.broadcasted_iota(jnp.int32, (rows, tiles), 1)
        expand = jnp.where(lax.shift_right_logical(which, 3) == owner, 1.0, 0.0)
        listed = jnp.dot(
            expand, cols_v[p, 0, 0].astype(F32), precision=lax.Precision.HIGHEST, preferred_element_type=F32
        )
        r = lax.broadcasted_iota(jnp.int32, (rows, cap), 0)
        c = lax.broadcasted_iota(jnp.int32, (rows, cap), 1)
        column = jnp.sum(jnp.where((r & 7) == c, listed, 0.0), axis=1, keepdims=True)
        rr = lax.broadcasted_iota(jnp.int32, (rows, columns), 0)
        cc = lax.broadcasted_iota(jnp.int32, (rows, columns), 1)
        hit = jnp.logical_and(cc == column.astype(jnp.int32), (rr & 7) < cap)
        return jnp.where(hit, 1.0, 0.0).astype(BF16)

    def occultation_weights(p):
        shape = (rows, slot_v.shape[3])
        m = lax.broadcasted_iota(jnp.int32, shape, 0)
        key = jnp.where((m & 7) < cap, lax.shift_right_logical(m, 3) * cap + (m & 7), -1)
        counts = oc_v[p]
        total = jnp.zeros(shape, F32)
        for k in range(slot_v.shape[2]):
            w = jnp.where(counts > k, ow_v[p, 0, k : k + 1, :], 0.0)
            total = total + jnp.where(key == slot_v[p, 0, k : k + 1, :], w, 0.0)
        return total

    def mixed_spread():
        f = field[...]
        around = pltpu.roll(f, 1, 1) + pltpu.roll(f, ext - 1, 1)
        spread = f + rates[...] * (around - 2.0 * f)
        xh, xl = split(spread)
        return mm(mix_a[...], jnp.concatenate([xh, xl], axis=0), NN) + mm(mix_b[...], xh, NN)

    def boundary_of(p):
        pos = position[...]
        inner = pos & (LANES - 1)
        outer = lax.shift_right_logical(pos, 7)

        def look(a):
            for d in range(3):
                pltpu.make_async_remote_copy(
                    src_ref=surf.at[p],
                    dst_ref=tab.at[p, d, a],
                    send_sem=surf_send.at[p, d, 0],
                    recv_sem=surf_recv.at[p, d, a],
                    device_id=(s, right),
                    device_id_type=MESH,
                ).wait_recv()
            found = picked[...]
            for b in range(blocks):
                at = slice(b * LANES, (b + 1) * LANES)
                table = jnp.concatenate(
                    [
                        jnp.broadcast_to(tab[p, 0, a, :, at], (blocks * rk, LANES)),
                        jnp.broadcast_to(tab[p, 1, a, :, at], (rk, LANES)),
                        jnp.broadcast_to(tab[p, 2, a, :, at], (rk, LANES)),
                    ],
                    axis=0,
                )
                got = jnp.take_along_axis(table, inner, axis=1, mode="promise_in_bounds")
                found = jnp.where(outer == a * blocks + b, got, found)
            picked[...] = found

        picked[...] = jnp.zeros(picked.shape, F32)
        look(0)

        @pl.when(is_ocean)
        def _():
            for a in range(1, ocean):
                look(a)

        terms = picked[...] * weight[...]
        sums = [jnp.sum(terms[b * rk : (b + 1) * rk], axis=0, keepdims=True) for b in range(blocks + 2)]
        sums[blocks] = jnp.where(row_lane < LANES // 2, sums[blocks], sums[blocks + 1])
        return [
            sums[b] - field[levels - 1 : levels, b * LANES : (b + 1) * LANES] for b in range(blocks + 1)
        ]

    def coupling_step(p):
        product = mixed_spread()
        boundary = boundary_of(p)
        push = jnp.concatenate([gain[...] * row for row in boundary], axis=1)
        push = push + forcing[...]
        field[...] = jnp.where(live, product + push, field[...])
        for _ in range(SUBS - 1):
            field[...] = jnp.where(live, mixed_spread() + push, field[...])

    def column_copy(p, other, source):
        return pltpu.make_async_remote_copy(
            src_ref=chosen_out.at[p, other],
            dst_ref=chosen_in.at[p, source],
            send_sem=col_send.at[p, other],
            recv_sem=col_recv.at[p, source],
            device_id=(s, other),
            device_id_type=MESH,
        )

    def send_columns(p, pick):
        fh, fl = split(field[:, 0:columns])
        taken = mm(pick, fh, NT) + mm(pick, fl, NT)
        projected = dot3(taken, refr_v[...]).reshape(tiles, 8, levels)
        chosen_out[p] = projected
        over_tiles(lambda other: column_copy(p, other, t).start())
        chosen_in[p, t] = chosen_out[p, t]

    own = parts_out.shape[2]

    def part_copy(p, other, source):
        return pltpu.make_async_remote_copy(
            src_ref=parts_out.at[p, other],
            dst_ref=parts_in.at[p, source],
            send_sem=red_send.at[p, other],
            recv_sem=red_recv.at[p, source],
            device_id=(other, t),
            device_id_type=MESH,
        )

    def others():
        return [lax.rem(s + d, sections) for d in range(1, sections)]

    def send_parts(p, w):
        over_tiles(lambda other: column_copy(p, other, other).wait_recv())
        part = dot3(w, chosen_in[p].reshape(rows, levels), TN)
        parts_out[p] = part.reshape(sections, own, levels)
        for other in others():
            part_copy(p, other, s).start()
        parts_in[p, s] = parts_out[p, s]

    def depart(p):
        for other in others():
            part_copy(p, other, other).wait_recv()
        total = parts_in[p, 0]
        for a in range(1, sections):
            total = total + parts_in[p, a]
        dep_v[p] = obs_v[p] - dot3(total, abel_v[...])

    picks = [selector(p) for p in range(STEPS)]
    occ = [occultation_weights(p) for p in range(STEPS)]

    for copy in packs:
        copy.wait_recv()
    gap = jnp.zeros((LANES - 2 * HALO, levels), F32)

    def pad(i):
        at = slice(i * HALO, (i + 1) * HALO)
        return jnp.concatenate([pack_in[0, at, :], gap, pack_in[1, at, :]], axis=0).T

    field[:, columns:ext] = pad(0)
    rates[:, columns:ext] = pad(1)
    forcing[:, columns:ext] = pad(2)
    for i in range(2):
        at = slice((blocks + i) * rk, (blocks + i + 1) * rk)
        position[at, :] = pack_in[i, 3 * HALO : 3 * HALO + rk, :].astype(jnp.int32)
        weight[at, :] = pack_in[i, 3 * HALO + rk : PACK, :]

    coupling_step(0)
    surf[1] = field[levels - 1 : levels, 0:columns]
    surf_each(1, lambda copy: copy.start())
    send_columns(0, picks[0])
    coupling_step(1)
    stores = [pltpu.make_async_copy(field.at[:, 0:columns], out_state.at[0], store_sem.at[0])]
    stores[0].start()
    send_columns(1, picks[1])
    send_parts(0, occ[0])
    send_parts(1, occ[1])
    depart(0)
    depart(1)
    stores.append(pltpu.make_async_copy(dep_v, out_departures, store_sem.at[1]))
    stores[1].start()

    for copy in packs:
        copy.wait_send()
    for p in range(STEPS):
        surf_each(p, lambda copy: copy.wait_send())
        over_tiles(lambda other: column_copy(p, other, t).wait_send())
        for other in others():
            part_copy(p, other, s).wait_send()
    for store in stores:
        store.wait()


def shards(sections, tiles, *args):
    (state, tendency, diffusion, mixing, coupling, remap_index, remap_weight, active_cols, send_cols) = args[:9]
    (occ_slot, occ_weight, occ_count, refraction, abel_matrix, observed) = args[9:]
    levels, columns = state.shape[1:]
    rk = remap_index.shape[1]
    ext = columns + LANES
    slots = (columns // LANES + 2) * rk
    own = observed.shape[1]
    heights = abel_matrix.shape[1]
    dma = pltpu.SemaphoreType.DMA
    any_spec = pl.BlockSpec(memory_space=pl.ANY)
    smem = pl.BlockSpec(memory_space=pltpu.SMEM)
    specs = [any_spec] * len(args)
    specs[7] = smem
    scratch = [
        pltpu.VMEM((levels, ext), F32),
        pltpu.VMEM((levels, ext), F32),
        pltpu.VMEM((levels, ext), F32),
        pltpu.VMEM((levels, columns), BF16),
        pltpu.VMEM((levels, columns), BF16),
        pltpu.VMEM((levels, levels), F32),
        pltpu.VMEM(coupling.shape, F32),
        pltpu.VMEM((rk, columns), jnp.int32),
        pltpu.VMEM((rk, columns), F32),
        pltpu.VMEM(send_cols.shape, jnp.int32),
        pltpu.VMEM(occ_slot.shape, jnp.int32),
        pltpu.VMEM(occ_weight.shape, F32),
        pltpu.VMEM(occ_count.shape, jnp.int32),
        pltpu.VMEM((levels, levels), F32),
        pltpu.VMEM(abel_matrix.shape, F32),
        pltpu.VMEM(observed.shape, F32),
        pltpu.VMEM(observed.shape, F32),
        pltpu.VMEM((levels, 2 * levels), BF16),
        pltpu.VMEM((levels, levels), BF16),
        pltpu.VMEM((levels, LANES), F32),
        pltpu.VMEM((slots, LANES), jnp.int32),
        pltpu.VMEM((slots, LANES), F32),
        pltpu.VMEM((slots, LANES), F32),
        pltpu.VMEM((STEPS, 1, columns), F32),
        pltpu.VMEM((STEPS, 3, sections - 1, 1, columns), F32),
        pltpu.VMEM((2, PACK, LANES), F32),
        pltpu.VMEM((2, PACK, LANES), F32),
        pltpu.VMEM((STEPS, tiles, 8, levels), F32),
        pltpu.VMEM((STEPS, tiles, 8, levels), F32),
        pltpu.VMEM((STEPS, sections, own, levels), F32),
        pltpu.VMEM((STEPS, sections, own, levels), F32),
        dma((14,)),
        dma((2,)),
        dma((2,)),
        dma((2,)),
        dma((STEPS, 3, sections - 1)),
        dma((STEPS, 3, sections - 1)),
        dma((STEPS, tiles)),
        dma((STEPS, tiles)),
        dma((STEPS, sections)),
        dma((STEPS, sections)),
    ]
    return pl.pallas_call(
        functools.partial(kernel, sections, tiles),
        out_shape=(
            jax.ShapeDtypeStruct(state.shape, F32),
            jax.ShapeDtypeStruct((STEPS, own, heights), F32),
        ),
        in_specs=specs,
        out_specs=(any_spec, any_spec),
        scratch_shapes=scratch,
        compiler_params=pltpu.CompilerParams(
            collective_id=0, has_side_effects=True, vmem_limit_bytes=32 * 1024 * 1024
        ),
        cost_estimate=pl.CostEstimate(flops=700_000_000, bytes_accessed=1_500_000, transcendentals=0),
    )(*args)


def solution(mesh):
    return jax.shard_map(
        functools.partial(shards, mesh.shape["sec"], mesh.shape["tile"]),
        mesh=mesh,
        in_specs=(
            P("sec", None, "tile"),
            P("sec", None, "tile"),
            P("sec", None, "tile"),
            P("sec", None, None),
            P("sec", None),
            P("sec", None, "tile"),
            P("sec", None, "tile"),
            P(),
            P(None, "sec", "tile", None, None),
            P(None, "sec", None, "tile"),
            P(None, "sec", None, "tile"),
            P(None, "sec", "tile"),
            P("sec", None, None),
            P(),
            P(None, ("sec", "tile"), None),
        ),
        out_specs=(P("sec", None, "tile"), P(None, ("sec", "tile"), None)),
        check_vma=False,
    )
```

time: 169 us -> 37.1 us (0.22)
  waiting for transfers between devices: 53 us -> 0 us
  starting transfers between devices: 46.3 us -> 0 us
  Pallas kernels: 0 us -> 25.6 us
  local copies, waits for them, and re-layouts: 35 us -> 10.3 us
  between operations: 14.5 us -> 0.7 us
  blocking collectives: 10.3 us -> 0 us
  matrix products: 5.53 us -> 0 us
  other arithmetic: 3.5 us -> 0 us
    ppermute x16 -> x0, starting transfers between devices: 40.2 us -> none  [the longest x8 36.7 us: extended(): lax.ppermute(lax.slice_in_dim(block, 0, width, axis=dim), axis, backward)]
    reduce_scatter x2 -> x0, waiting for transfers between devices: 37.3 us -> none  [observe(): owned = lax.psum_scatter(bending, 'sec', scatter_dimension=0, tiled=True)]
    gather x8 -> x0, local copies, waits for them, and re-layouts: 26.8 us -> none  [the longest x4 23.6 us: shards(): picked = jnp.take(surfaces.reshape(-1), position)]
    pallas_call x0 -> x1, Pallas kernels: none -> 25.6 us  [shards(): pl.pallas_call(functools.partial(kernel, sections, tiles), out_shape=(jax...]
    all_gather x2 -> x0, blocking collectives: 10.3 us -> none  [shards(): surfaces = lax.all_gather(surface[None], 'sec', axis=0, tiled=True)]
    ppermute x16 -> x0, waiting for transfers between devices: 9.04 us -> none  [the longest x8 9.02 us: extended(): lax.ppermute(lax.slice_in_dim(block, block.shape[dim] - width, None, axis...]
    all_to_all x1 -> x0, waiting for transfers between devices: 6.63 us -> none  [shards(): lax.all_to_all(jnp.stack(outgoing, 1), 'tile', split_axis=0, concat_axis=...]
    all_to_all x1 -> x0, starting transfers between devices: 6.06 us -> none  [shards(): lax.all_to_all(jnp.stack(outgoing, 1), 'tile', split_axis=0, concat_axis=...]
  transfers between devices with their start and end apart: 19 -> 0, of which waited for: 10 -> 0; matrix products, arithmetic and copies ran while one was open for 10% -> 0% of each run, Pallas kernels for 0% -> 0%
where the time goes in v1:
time: 37.1 us; the launch traced here: 36.6 us
  Pallas kernels  25.6 us (69%)
  local copies, waits for them, and re-layouts  10.3 us (28%)
  between operations  0.7 us (2%)
    pallas_call x1, Pallas kernels, shards(): pl.pallas_call(functools.partial(kernel, sections, tiles), out_shape=(jax...  25.6 us
    unnamed x31, local copies, waits for them, and re-layouts  10.3 us

profile of v1, /device:TPU:0, one launch (start us, length us, event | category | flops | bytes accessed | tf_op | source)
XLA Modules:
  0.0 36.6 jit_solution(6009735673097664970)
XLA Ops:
  0.6 0.0 copy-start.11
  0.6 0.0 copy-start.13
  0.7 0.0 copy-start.7
  0.7 0.0 copy-start.12
  0.7 0.8 %copy.17.send_cols = s32[2,1,1,8,4]{4,3,2,1,0:T(8,128)S(1)} copy(s32[2,1,1,8,4]{3,4,2,1,0:T(4,128)} %param.23) | data formatting | bytes 512 | tf_op args[8]
  1.5 0.0 copy-done.11
  1.5 0.0 copy-done.13
  1.5 0.0 copy-done.7
  1.5 0.0 copy-done.12
  1.5 0.0 copy-start
  1.5 0.9 %copy-done = f32[1,128,512]{2,1,0:T(8,128)S(1)} copy-done((f32[1,128,512]{2,1,0:T(8,128)S(1)}, f32[1,128,512]{2,1,0:T(8,128)}, u32[]{:S(2)}) %copy-start) | copy-done | bytes 262168
  2.4 0.0 copy-start.1
  2.4 0.9 %copy-done.1 = bf16[1,128,512]{2,1,0:T(8,128)(2,1)S(1)} copy-done((bf16[1,128,512]{2,1,0:T(8,128)(2,1)S(1)}, bf16[1,128,512]{2,1,0:T(8,128)(2,1)}, u32[]{:S(2)}) %copy-start.1) | copy-done | bytes 131096
  3.3 0.0 copy-start.2
  3.3 0.9 %copy-done.2 = bf16[1,128,512]{2,1,0:T(8,128)(2,1)S(1)} copy-done((bf16[1,128,512]{2,1,0:T(8,128)(2,1)S(1)}, bf16[1,128,512]{2,1,0:T(8,128)(2,1)}, u32[]{:S(2)}) %copy-start.2) | copy-done | bytes 131096
  4.2 0.0 copy-start.3
  4.2 0.9 %copy-done.3 = f32[128,256]{1,0:T(8,128)S(1)} copy-done((f32[128,256]{1,0:T(8,128)S(1)}, f32[128,256]{1,0:T(8,128)}, u32[]{:S(2)}) %copy-start.3) | copy-done | bytes 131096
  5.1 0.0 copy-start.4
  5.1 0.8 %copy-done.4 = f32[1,128,128]{2,1,0:T(8,128)S(1)} copy-done((f32[1,128,128]{2,1,0:T(8,128)S(1)}, f32[1,128,128]{2,1,0:T(8,128)}, u32[]{:S(2)}) %copy-start.4) | copy-done | bytes 65560
  6.0 0.0 copy-start.5
  6.0 0.8 %copy-done.5 = f32[1,128,128]{2,1,0:T(8,128)S(1)} copy-done((f32[1,128,128]{2,1,0:T(8,128)S(1)}, f32[1,128,128]{2,1,0:T(8,128)}, u32[]{:S(2)}) %copy-start.5) | copy-done | bytes 65560
  6.8 0.0 copy-start.6
  6.8 0.8 %copy-done.6 = f32[2,16,256]{2,1,0:T(8,128)S(1)} copy-done((f32[2,16,256]{2,1,0:T(8,128)S(1)}, f32[2,16,256]{2,1,0:T(8,128)}, u32[]{:S(2)}) %copy-start.6) | copy-done | bytes 32792
  7.6 0.0 copy-start.8
  7.6 0.7 %copy-done.8 = f32[1,4,512]{2,1,0:T(4,128)S(1)} copy-done((f32[1,4,512]{2,1,0:T(4,128)S(1)}, f32[1,4,512]{2,1,0:T(4,128)}, u32[]{:S(2)}) %copy-start.8) | copy-done | bytes 8216
  8.3 0.0 copy-start.9
  8.3 0.7 %copy-done.9 = s32[2,1,8,64]{3,2,1,0:T(8,128)S(1)} copy-done((s32[2,1,8,64]{3,2,1,0:T(8,128)S(1)}, s32[2,1,8,64]{3,2,1,0:T(8,128)}, u32[]{:S(2)}) %copy-start.9) | copy-done | bytes 4120
  9.0 0.0 copy-start.10
  9.0 0.7 %copy-done.10 = f32[2,1,8,64]{3,2,1,0:T(8,128)S(1)} copy-done((f32[2,1,8,64]{3,2,1,0:T(8,128)S(1)}, f32[2,1,8,64]{3,2,1,0:T(8,128)}, u32[]{:S(2)}) %copy-start.10) | copy-done | bytes 4120
  9.7 25.6 %shard_map.158 = (f32[1,128,512]{2,1,0:T(8,128)S(1)}, f32[2,16,256]{2,1,0:T(8,128)S(1)}) custom-call(f32[1,128,512]{2,1,0:T(8,128)S(1)} %copy-done, bf16[1,128,512]{2,1,0:T(8,128)(2,1)S(1)} %copy-done.1, bf16[1,128,512]{2,1,0:T(8,128)(2,1)S(1)} %copy-done.2, f32[1,128,128]{2,1,0:T(8,128)S(1)} %copy-done.4, f32[1,128]{1,0:T(1,128)S(1)} %copy-done.12, ...), custom_call_target="tpu_custom_call" | custom-call | flops 700000000 | bytes 1500000 | tf_op jit(solution)/shard_map/pallas_call | solution.py:489
  35.3 0.7 %copy.20 = f32[1,128,512]{2,1,0:T(8,128)} copy(f32[1,128,512]{2,1,0:T(8,128)S(1)} %get-tuple-element.4) | data formatting | bytes 524288
  36.0 0.6 %copy.21 = f32[2,16,256]{2,1,0:T(8,128)} copy(f32[2,16,256]{2,1,0:T(8,128)S(1)} %get-tuple-element.5) | data formatting | bytes 65536
Async XLA Ops:
  0.6 0.8 %copy-start.11 = (s32[2,1,64]{2,1,0:T(1,128)S(1)}, s32[2,1,64]{2,1,0:T(1,128)}, u32[]{:S(2)}) copy-start(s32[2,1,64]{2,1,0:T(1,128)} %occ_count.1) | copy-start | bytes 1540
  0.6 0.8 %copy-start.13 = (s32[4]{0:T(128)S(1)}, s32[4]{0:T(128)}, u32[]{:S(2)}) copy-start(s32[4]{0:T(128)} %active_cols.1) | copy-start | bytes 52
  0.7 0.8 %copy-start.7 = (s32[1,4,512]{2,1,0:T(4,128)S(1)}, s32[1,4,512]{2,1,0:T(4,128)}, u32[]{:S(2)}) copy-start(s32[1,4,512]{2,1,0:T(4,128)} %remap_index.1) | copy-start | bytes 24580
  0.7 0.8 %copy-start.12 = (f32[1,128]{1,0:T(1,128)S(1)}, f32[1,128]{1,0:T(1,128)}, u32[]{:S(2)}) copy-start(f32[1,128]{1,0:T(1,128)} %coupling.1) | copy-start | bytes 1540
  1.5 1.0 %copy-start = (f32[1,128,512]{2,1,0:T(8,128)S(1)}, f32[1,128,512]{2,1,0:T(8,128)}, u32[]{:S(2)}) copy-start(f32[1,128,512]{2,1,0:T(8,128)} %state.1) | copy-start | bytes 786436
  2.4 0.9 %copy-start.1 = (bf16[1,128,512]{2,1,0:T(8,128)(2,1)S(1)}, bf16[1,128,512]{2,1,0:T(8,128)(2,1)}, u32[]{:S(2)}) copy-start(bf16[1,128,512]{2,1,0:T(8,128)(2,1)} %tendency.1) | copy-start | bytes 393220
  3.3 0.9 %copy-start.2 = (bf16[1,128,512]{2,1,0:T(8,128)(2,1)S(1)}, bf16[1,128,512]{2,1,0:T(8,128)(2,1)}, u32[]{:S(2)}) copy-start(bf16[1,128,512]{2,1,0:T(8,128)(2,1)} %diffusion.1) | copy-start | bytes 393220
  4.2 0.9 %copy-start.3 = (f32[128,256]{1,0:T(8,128)S(1)}, f32[128,256]{1,0:T(8,128)}, u32[]{:S(2)}) copy-start(f32[128,256]{1,0:T(8,128)} %abel_matrix.1) | copy-start | bytes 393220
  5.1 0.8 %copy-start.4 = (f32[1,128,128]{2,1,0:T(8,128)S(1)}, f32[1,128,128]{2,1,0:T(8,128)}, u32[]{:S(2)}) copy-start(f32[1,128,128]{2,1,0:T(8,128)} %mixing.1) | copy-start | bytes 196612
  6.0 0.8 %copy-start.5 = (f32[1,128,128]{2,1,0:T(8,128)S(1)}, f32[1,128,128]{2,1,0:T(8,128)}, u32[]{:S(2)}) copy-start(f32[1,128,128]{2,1,0:T(8,128)} %refraction.1) | copy-start | bytes 196612
  6.8 0.8 %copy-start.6 = (f32[2,16,256]{2,1,0:T(8,128)S(1)}, f32[2,16,256]{2,1,0:T(8,128)}, u32[]{:S(2)}) copy-start(f32[2,16,256]{2,1,0:T(8,128)} %observed.1) | copy-start | bytes 98308
  7.6 0.7 %copy-start.8 = (f32[1,4,512]{2,1,0:T(4,128)S(1)}, f32[1,4,512]{2,1,0:T(4,128)}, u32[]{:S(2)}) copy-start(f32[1,4,512]{2,1,0:T(4,128)} %remap_weight.1) | copy-start | bytes 24580
  8.3 0.7 %copy-start.9 = (s32[2,1,8,64]{3,2,1,0:T(8,128)S(1)}, s32[2,1,8,64]{3,2,1,0:T(8,128)}, u32[]{:S(2)}) copy-start(s32[2,1,8,64]{3,2,1,0:T(8,128)} %occ_slot.1) | copy-start | bytes 12292
  9.0 0.7 %copy-start.10 = (f32[2,1,8,64]{3,2,1,0:T(8,128)S(1)}, f32[2,1,8,64]{3,2,1,0:T(8,128)}, u32[]{:S(2)}) copy-start(f32[2,1,8,64]{3,2,1,0:T(8,128)} %occ_weight.1) | copy-start | bytes 12292

commit v2 on v1

--- a/solution.py
+++ b/solution.py
@@ -61,6 +61,7 @@
     field,
     rates,
     forcing,
+    drive,
     tend_v,
     diff_v,
     mix_v,
@@ -245,15 +246,19 @@
     )
     live = number < limit
 
-    cap = cols_v.shape[4]
+    cap = cols_v.shape[3]
     rows = tiles * 8
 
     def selector(p):
         which = lax.broadcasted_iota(jnp.int32, (rows, tiles), 0)
         owner = lax.broadcasted_iota(jnp.int32, (rows, tiles), 1)
         expand = jnp.where(lax.shift_right_logical(which, 3) == owner, 1.0, 0.0)
-        listed = jnp.dot(
-            expand, cols_v[p, 0, 0].astype(F32), precision=lax.Precision.HIGHEST, preferred_element_type=F32
+        listed = lax.dot_general(
+            expand,
+            cols_v[p, 0, 0].astype(F32),
+            (NT, ((), ())),
+            precision=lax.Precision.HIGHEST,
+            preferred_element_type=F32,
         )
         r = lax.broadcasted_iota(jnp.int32, (rows, cap), 0)
         c = lax.broadcasted_iota(jnp.int32, (rows, cap), 1)
@@ -332,8 +337,13 @@
         push = jnp.concatenate([gain[...] * row for row in boundary], axis=1)
         push = push + forcing[...]
         field[...] = jnp.where(live, product + push, field[...])
-        for _ in range(SUBS - 1):
-            field[...] = jnp.where(live, mixed_spread() + push, field[...])
+        drive[...] = push
+
+        def substep(_, carry):
+            field[...] = jnp.where(live, mixed_spread() + drive[...], field[...])
+            return carry
+
+        lax.fori_loop(0, SUBS - 1, substep, 0)
 
     def column_copy(p, other, source):
         return pltpu.make_async_remote_copy(
@@ -384,9 +394,6 @@
             total = total + parts_in[p, a]
         dep_v[p] = obs_v[p] - dot3(total, abel_v[...])
 
-    picks = [selector(p) for p in range(STEPS)]
-    occ = [occultation_weights(p) for p in range(STEPS)]
-
     for copy in packs:
         copy.wait_recv()
     gap = jnp.zeros((LANES - 2 * HALO, levels), F32)
@@ -406,13 +413,13 @@
     coupling_step(0)
     surf[1] = field[levels - 1 : levels, 0:columns]
     surf_each(1, lambda copy: copy.start())
-    send_columns(0, picks[0])
+    send_columns(0, selector(0))
     coupling_step(1)
     stores = [pltpu.make_async_copy(field.at[:, 0:columns], out_state.at[0], store_sem.at[0])]
     stores[0].start()
-    send_columns(1, picks[1])
-    send_parts(0, occ[0])
-    send_parts(1, occ[1])
+    send_columns(1, selector(1))
+    send_parts(0, occultation_weights(0))
+    send_parts(1, occultation_weights(1))
     depart(0)
     depart(1)
     stores.append(pltpu.make_async_copy(dep_v, out_departures, store_sem.at[1]))
@@ -432,6 +439,8 @@
 def shards(sections, tiles, *args):
     (state, tendency, diffusion, mixing, coupling, remap_index, remap_weight, active_cols, send_cols) = args[:9]
     (occ_slot, occ_weight, occ_count, refraction, abel_matrix, observed) = args[9:]
+    send_cols = jnp.swapaxes(send_cols, 3, 4)
+    args = args[:8] + (send_cols,) + args[9:]
     levels, columns = state.shape[1:]
     rk = remap_index.shape[1]
     ext = columns + LANES
@@ -439,11 +448,12 @@
     own = observed.shape[1]
     heights = abel_matrix.shape[1]
     dma = pltpu.SemaphoreType.DMA
-    any_spec = pl.BlockSpec(memory_space=pl.ANY)
+    any_spec = pl.BlockSpec(memory_space=pltpu.HBM)
     smem = pl.BlockSpec(memory_space=pltpu.SMEM)
     specs = [any_spec] * len(args)
     specs[7] = smem
     scratch = [
+        pltpu.VMEM((levels, ext), F32),
         pltpu.VMEM((levels, ext), F32),
         pltpu.VMEM((levels, ext), F32),
         pltpu.VMEM((levels, ext), F32),
@@ -496,7 +506,7 @@
         out_specs=(any_spec, any_spec),
         scratch_shapes=scratch,
         compiler_params=pltpu.CompilerParams(
-            collective_id=0, has_side_effects=True, vmem_limit_bytes=32 * 1024 * 1024
+            collective_id=0, has_side_effects=True, vmem_limit_bytes=64 * 1024 * 1024 - 64 * 1024
         ),
         cost_estimate=pl.CostEstimate(flops=700_000_000, bytes_accessed=1_500_000, transcendentals=0),
     )(*args)

time: 37.1 us -> 29.2 us (0.79)
  local copies, waits for them, and re-layouts: 10.3 us -> 2.3 us
  Pallas kernels: 25.6 us -> 26.1 us
    unnamed x31 -> x4, local copies, waits for them, and re-layouts: 10.3 us -> 2.3 us
    pallas_call x1, Pallas kernels: 25.6 us -> 26.1 us  [shards(): pl.pallas_call(functools.partial(kernel, sections, tiles), out_shape=(jax...]
where the time goes in v2:
time: 29.2 us; the launch traced here: 29 us
  Pallas kernels  26.1 us (89%)
  local copies, waits for them, and re-layouts  2.3 us (8%)
  between operations  0.65 us (2%)
    pallas_call x1, Pallas kernels, shards(): pl.pallas_call(functools.partial(kernel, sections, tiles), out_shape=(jax...  26.1 us
    unnamed x4, local copies, waits for them, and re-layouts  2.3 us

profile of v2, /device:TPU:0, one launch (start us, length us, event | category | flops | bytes accessed | tf_op | source)
XLA Modules:
  0.0 29.0 jit_solution(12997541583174068262)
XLA Ops:
  0.6 26.1 %shard_map.158 = (f32[1,128,512]{2,1,0:T(8,128)}, f32[2,16,256]{2,1,0:T(8,128)}) custom-call(f32[1,128,512]{2,1,0:T(8,128)} %state.1, bf16[1,128,512]{2,1,0:T(8,128)(2,1)} %tendency.1, bf16[1,128,512]{2,1,0:T(8,128)(2,1)} %diffusion.1, f32[1,128,128]{2,1,0:T(8,128)} %mixing.1, f32[1,128]{1,0:T(1,128)} %coupling.1, s32[1,4,512]{2,1,0:T(4,128)} %remap_index.1, ...), custom_call_target="tpu_custom_call" | custom-call | flops 700000000 | bytes 1500000 | tf_op jit(solution)/shard_map/pallas_call | solution.py:499
  26.7 0.0 copy-start
  26.7 1.7 %copy.19 = f32[1,128,512]{2,1,0:T(8,128)} copy(f32[1,128,512]{2,1,0:T(8,128)} %get-tuple-element.4) | data formatting | bytes 524288
  28.4 0.0 copy-done
  28.4 0.6 %copy.20 = f32[2,16,256]{2,1,0:T(8,128)} copy(f32[2,16,256]{2,1,0:T(8,128)S(1)} %copy-done) | data formatting | bytes 65536
Async XLA Ops:
  26.7 1.7 %copy-start = (f32[2,16,256]{2,1,0:T(8,128)S(1)}, f32[2,16,256]{2,1,0:T(8,128)}, u32[]{:S(2)}) copy-start(f32[2,16,256]{2,1,0:T(8,128)} %get-tuple-element.5) | copy-start | bytes 98308

commit v3 on v2

--- a/solution.py
+++ b/solution.py
@@ -78,6 +78,7 @@
     dep_v,
     mix_a,
     mix_b,
+    pick_v,
     gain,
     position,
     weight,
@@ -130,9 +131,6 @@
         (observed, obs_v),
     ]
     loads = [pltpu.make_async_copy(a, b, load_sem.at[i]) for i, (a, b) in enumerate(loads)]
-    for load in loads:
-        load.start()
-
     def over_tiles(body):
         if tiles <= 8:
             for d in range(1, tiles):
@@ -159,6 +157,9 @@
     def _():
         greet(ocean, left)
         greet(ocean, right)
+
+    for load in loads:
+        load.start()
 
     lane = lax.broadcasted_iota(jnp.int32, (levels, LANES), 1)
     row_lane = lax.broadcasted_iota(jnp.int32, (1, LANES), 1)
@@ -279,12 +280,16 @@
             total = total + jnp.where(key == slot_v[p, 0, k : k + 1, :], w, 0.0)
         return total
 
-    def mixed_spread():
+    def spread_halves():
         f = field[...]
         around = pltpu.roll(f, 1, 1) + pltpu.roll(f, ext - 1, 1)
         spread = f + rates[...] * (around - 2.0 * f)
         xh, xl = split(spread)
-        return mm(mix_a[...], jnp.concatenate([xh, xl], axis=0), NN) + mm(mix_b[...], xh, NN)
+        return jnp.concatenate([xh, xl], axis=0), xh
+
+    def mixed_spread():
+        xx, xh = spread_halves()
+        return mm(mix_a[...], xx, NN) + mm(mix_b[...], xh, NN)
 
     def boundary_of(p):
         pos = position[...]
@@ -343,7 +348,18 @@
             field[...] = jnp.where(live, mixed_spread() + drive[...], field[...])
             return carry
 
-        lax.fori_loop(0, SUBS - 1, substep, 0)
+        if p == STEPS - 1:
+            lax.fori_loop(0, SUBS - 1, substep, 0)
+            return
+        lax.fori_loop(0, SUBS - 2, substep, 0)
+        xx, xh = spread_halves()
+        low = slice(levels - 8, levels)
+        row = mm(mix_a[low, :], xx, NN) + mm(mix_b[low, :], xh, NN) + drive[low, :]
+        row = jnp.where(live, row, field[low, :])
+        surf[p + 1] = row[7:8, 0:columns]
+        surf_each(p + 1, lambda copy: copy.start())
+        product = mm(mix_a[...], xx, NN) + mm(mix_b[...], xh, NN)
+        field[...] = jnp.where(live, product + drive[...], field[...])
 
     def column_copy(p, other, source):
         return pltpu.make_async_remote_copy(
@@ -355,7 +371,8 @@
             device_id_type=MESH,
         )
 
-    def send_columns(p, pick):
+    def send_columns(p):
+        pick = pick_v[p]
         fh, fl = split(field[:, 0:columns])
         taken = mm(pick, fh, NT) + mm(pick, fl, NT)
         projected = dot3(taken, refr_v[...]).reshape(tiles, 8, levels)
@@ -394,6 +411,9 @@
             total = total + parts_in[p, a]
         dep_v[p] = obs_v[p] - dot3(total, abel_v[...])
 
+    for p in range(STEPS):
+        pick_v[p] = selector(p)
+
     for copy in packs:
         copy.wait_recv()
     gap = jnp.zeros((LANES - 2 * HALO, levels), F32)
@@ -411,29 +431,41 @@
         weight[at, :] = pack_in[i, 3 * HALO + rk : PACK, :]
 
     coupling_step(0)
-    surf[1] = field[levels - 1 : levels, 0:columns]
-    surf_each(1, lambda copy: copy.start())
-    send_columns(0, selector(0))
+    send_columns(0)
     coupling_step(1)
-    stores = [pltpu.make_async_copy(field.at[:, 0:columns], out_state.at[0], store_sem.at[0])]
-    stores[0].start()
-    send_columns(1, selector(1))
-    send_parts(0, occultation_weights(0))
-    send_parts(1, occultation_weights(1))
-    depart(0)
-    depart(1)
-    stores.append(pltpu.make_async_copy(dep_v, out_departures, store_sem.at[1]))
-    stores[1].start()
-
+    store = pltpu.make_async_copy(field.at[:, 0:columns], out_state.at[0], store_sem.at[0])
+    store.start()
+    send_columns(1)
+    occ = [occultation_weights(p) for p in range(STEPS)]
+    send_parts(0, occ[0])
     for copy in packs:
         copy.wait_send()
     for p in range(STEPS):
         surf_each(p, lambda copy: copy.wait_send())
-        over_tiles(lambda other: column_copy(p, other, t).wait_send())
+    over_tiles(lambda other: column_copy(0, other, t).wait_send())
+    depart(0)
+    send_parts(1, occ[1])
+    over_tiles(lambda other: column_copy(1, other, t).wait_send())
+    for p in range(STEPS):
         for other in others():
             part_copy(p, other, s).wait_send()
-    for store in stores:
-        store.wait()
+    store.wait()
+    depart(1)
+    last = pltpu.make_async_copy(dep_v, out_departures, store_sem.at[1])
+    last.start()
+    last.wait()
+
+
+def hand_over(state, departures, out_state, out_departures, sem):
+    rows = state.shape[1] // 4
+    copies = [pltpu.make_async_copy(departures, out_departures, sem.at[4])]
+    for i in range(4):
+        at = pl.ds(i * rows, rows)
+        copies.append(pltpu.make_async_copy(state.at[:, at], out_state.at[:, at], sem.at[i]))
+    for copy in copies:
+        copy.start()
+    for copy in copies:
+        copy.wait()
 
 
 def shards(sections, tiles, *args):
@@ -473,6 +505,7 @@
         pltpu.VMEM(observed.shape, F32),
         pltpu.VMEM((levels, 2 * levels), BF16),
         pltpu.VMEM((levels, levels), BF16),
+        pltpu.VMEM((STEPS, tiles * 8, columns), BF16),
         pltpu.VMEM((levels, LANES), F32),
         pltpu.VMEM((slots, LANES), jnp.int32),
         pltpu.VMEM((slots, LANES), F32),
@@ -496,7 +529,7 @@
         dma((STEPS, sections)),
         dma((STEPS, sections)),
     ]
-    return pl.pallas_call(
+    made = pl.pallas_call(
         functools.partial(kernel, sections, tiles),
         out_shape=(
             jax.ShapeDtypeStruct(state.shape, F32),
@@ -510,6 +543,15 @@
         ),
         cost_estimate=pl.CostEstimate(flops=700_000_000, bytes_accessed=1_500_000, transcendentals=0),
     )(*args)
+    return pl.pallas_call(
+        hand_over,
+        out_shape=tuple(jax.ShapeDtypeStruct(x.shape, x.dtype) for x in made),
+        in_specs=[any_spec] * 2,
+        out_specs=(any_spec, any_spec),
+        scratch_shapes=[dma((5,))],
+        cost_estimate=pl.CostEstimate(flops=0, bytes_accessed=600_000, transcendentals=0),
+        compiler_params=pltpu.CompilerParams(vmem_limit_bytes=64 * 1024 * 1024 - 64 * 1024),
+    )(*made)
 
 
 def solution(mesh):

time: 29.2 us -> 37.5 us (1.28)
  Pallas kernels: 26.1 us -> 36.7 us
  local copies, waits for them, and re-layouts: 2.3 us -> 0 us
    pallas_call x0 -> x1, Pallas kernels: none -> 10.1 us  [shards(): pl.pallas_call(hand_over, out_shape=tuple((jax.ShapeDtypeStruct(x.shape,...]
    unnamed x4 -> x0, local copies, waits for them, and re-layouts: 2.3 us -> none
    pallas_call x1, Pallas kernels: 26.1 us -> 26.6 us  [shards(): pl.pallas_call(functools.partial(kernel, sections, tiles), out_shape=(jax...]
where the time goes in v3:
time: 37.5 us; the launch traced here: 37.3 us
  Pallas kernels  36.7 us (98%)
  between operations  0.64 us (2%)
    pallas_call x1, Pallas kernels, shards(): pl.pallas_call(functools.partial(kernel, sections, tiles), out_shape=(jax...  26.6 us
    pallas_call x1, Pallas kernels, shards(): pl.pallas_call(hand_over, out_shape=tuple((jax.ShapeDtypeStruct(x.shape,...  10.1 us

profile of v3, /device:TPU:0, one launch (start us, length us, event | category | flops | bytes accessed | tf_op | source)
XLA Modules:
  0.0 37.3 jit_solution(17370819742509945731)
XLA Ops:
  0.6 26.6 %shard_map.158 = (f32[1,128,512]{2,1,0:T(8,128)}, f32[2,16,256]{2,1,0:T(8,128)}) custom-call(f32[1,128,512]{2,1,0:T(8,128)} %state.1, bf16[1,128,512]{2,1,0:T(8,128)(2,1)} %tendency.1, bf16[1,128,512]{2,1,0:T(8,128)(2,1)} %diffusion.1, f32[1,128,128]{2,1,0:T(8,128)} %mixing.1, f32[1,128]{1,0:T(1,128)} %coupling.1, s32[1,4,512]{2,1,0:T(4,128)} %remap_index.1, ...), custom_call_target="tpu_custom_call" | custom-call | flops 700000000 | bytes 1500000 | tf_op jit(solution)/shard_map/pallas_call | solution.py:532
  27.3 10.1 %shard_map.159 = (f32[1,128,512]{2,1,0:T(8,128)}, f32[2,16,256]{2,1,0:T(8,128)}) custom-call(f32[1,128,512]{2,1,0:T(8,128)} %get-tuple-element.4.state, f32[2,16,256]{2,1,0:T(8,128)} %get-tuple-element.5.departures), custom_call_target="tpu_custom_call" | custom-call | bytes 600000 | tf_op jit(solution)/shard_map/pallas_call | solution.py:546

commit v4 on v2

--- a/solution.py
+++ b/solution.py
@@ -78,6 +78,8 @@
     dep_v,
     mix_a,
     mix_b,
+    pick_v,
+    occ_v,
     gain,
     position,
     weight,
@@ -130,9 +132,6 @@
         (observed, obs_v),
     ]
     loads = [pltpu.make_async_copy(a, b, load_sem.at[i]) for i, (a, b) in enumerate(loads)]
-    for load in loads:
-        load.start()
-
     def over_tiles(body):
         if tiles <= 8:
             for d in range(1, tiles):
@@ -159,6 +158,9 @@
     def _():
         greet(ocean, left)
         greet(ocean, right)
+
+    for load in loads:
+        load.start()
 
     lane = lax.broadcasted_iota(jnp.int32, (levels, LANES), 1)
     row_lane = lax.broadcasted_iota(jnp.int32, (1, LANES), 1)
@@ -279,12 +281,16 @@
             total = total + jnp.where(key == slot_v[p, 0, k : k + 1, :], w, 0.0)
         return total
 
-    def mixed_spread():
+    def spread_halves():
         f = field[...]
         around = pltpu.roll(f, 1, 1) + pltpu.roll(f, ext - 1, 1)
         spread = f + rates[...] * (around - 2.0 * f)
         xh, xl = split(spread)
-        return mm(mix_a[...], jnp.concatenate([xh, xl], axis=0), NN) + mm(mix_b[...], xh, NN)
+        return jnp.concatenate([xh, xl], axis=0), xh
+
+    def mixed_spread():
+        xx, xh = spread_halves()
+        return mm(mix_a[...], xx, NN) + mm(mix_b[...], xh, NN)
 
     def boundary_of(p):
         pos = position[...]
@@ -343,7 +349,19 @@
             field[...] = jnp.where(live, mixed_spread() + drive[...], field[...])
             return carry
 
-        lax.fori_loop(0, SUBS - 1, substep, 0)
+        lax.fori_loop(0, SUBS - 2, substep, 0)
+        xx, xh = spread_halves()
+
+        @pl.when(p < STEPS - 1)
+        def _():
+            low = slice(levels - 8, levels)
+            row = mm(mix_a[low, :], xx, NN) + mm(mix_b[low, :], xh, NN) + drive[low, :]
+            row = jnp.where(live, row, field[low, :])
+            surf[p + 1] = row[7:8, 0:columns]
+            surf_each(p + 1, lambda copy: copy.start())
+
+        product = mm(mix_a[...], xx, NN) + mm(mix_b[...], xh, NN)
+        field[...] = jnp.where(live, product + drive[...], field[...])
 
     def column_copy(p, other, source):
         return pltpu.make_async_remote_copy(
@@ -355,7 +373,8 @@
             device_id_type=MESH,
         )
 
-    def send_columns(p, pick):
+    def send_columns(p):
+        pick = pick_v[p]
         fh, fl = split(field[:, 0:columns])
         taken = mm(pick, fh, NT) + mm(pick, fl, NT)
         projected = dot3(taken, refr_v[...]).reshape(tiles, 8, levels)
@@ -394,6 +413,12 @@
             total = total + parts_in[p, a]
         dep_v[p] = obs_v[p] - dot3(total, abel_v[...])
 
+    def list_columns(p, carry):
+        pick_v[p] = selector(p)
+        return carry
+
+    lax.fori_loop(0, STEPS, list_columns, 0)
+
     for copy in packs:
         copy.wait_recv()
     gap = jnp.zeros((LANES - 2 * HALO, levels), F32)
@@ -410,30 +435,52 @@
         position[at, :] = pack_in[i, 3 * HALO : 3 * HALO + rk, :].astype(jnp.int32)
         weight[at, :] = pack_in[i, 3 * HALO + rk : PACK, :]
 
-    coupling_step(0)
-    surf[1] = field[levels - 1 : levels, 0:columns]
-    surf_each(1, lambda copy: copy.start())
-    send_columns(0, selector(0))
-    coupling_step(1)
-    stores = [pltpu.make_async_copy(field.at[:, 0:columns], out_state.at[0], store_sem.at[0])]
-    stores[0].start()
-    send_columns(1, selector(1))
-    send_parts(0, occultation_weights(0))
-    send_parts(1, occultation_weights(1))
-    depart(0)
-    depart(1)
-    stores.append(pltpu.make_async_copy(dep_v, out_departures, store_sem.at[1]))
-    stores[1].start()
-
-    for copy in packs:
-        copy.wait_send()
-    for p in range(STEPS):
-        surf_each(p, lambda copy: copy.wait_send())
+    store = pltpu.make_async_copy(field.at[:, 0:columns], out_state.at[0], store_sem.at[0])
+
+    def period(p, carry):
+        coupling_step(p)
+
+        @pl.when(p == STEPS - 1)
+        def _():
+            store.start()
+
+        send_columns(p)
+        return carry
+
+    lax.fori_loop(0, STEPS, period, 0)
+
+    def weigh(p, carry):
+        occ_v[p] = occultation_weights(p)
+        return carry
+
+    lax.fori_loop(0, STEPS, weigh, 0)
+
+    def gather_parts(p, carry):
+        send_parts(p, occ_v[p])
+
+        @pl.when(p == 0)
+        def _():
+            for copy in packs:
+                copy.wait_send()
+            for q in range(STEPS):
+                surf_each(q, lambda copy: copy.wait_send())
+
         over_tiles(lambda other: column_copy(p, other, t).wait_send())
+        return carry
+
+    lax.fori_loop(0, STEPS, gather_parts, 0)
+
+    def finish(p, carry):
+        depart(p)
         for other in others():
             part_copy(p, other, s).wait_send()
-    for store in stores:
-        store.wait()
+        return carry
+
+    lax.fori_loop(0, STEPS, finish, 0)
+    last = pltpu.make_async_copy(dep_v, out_departures, store_sem.at[1])
+    last.start()
+    store.wait()
+    last.wait()
 
 
 def shards(sections, tiles, *args):
@@ -473,6 +520,8 @@
         pltpu.VMEM(observed.shape, F32),
         pltpu.VMEM((levels, 2 * levels), BF16),
         pltpu.VMEM((levels, levels), BF16),
+        pltpu.VMEM((STEPS, tiles * 8, columns), BF16),
+        pltpu.VMEM((STEPS, tiles * 8, occ_slot.shape[3]), F32),
         pltpu.VMEM((levels, LANES), F32),
         pltpu.VMEM((slots, LANES), jnp.int32),
         pltpu.VMEM((slots, LANES), F32),

time: 29.2 us -> 28.9 us (0.990)
  Pallas kernels: 26.1 us -> 25.8 us
    pallas_call x1, Pallas kernels: 26.1 us -> 25.8 us  [shards(): pl.pallas_call(functools.partial(kernel, sections, tiles), out_shape=(jax...]
where the time goes in v4:
time: 28.9 us; the launch traced here: 28.7 us
  Pallas kernels  25.8 us (89%)
  local copies, waits for them, and re-layouts  2.3 us (8%)
  between operations  0.65 us (2%)
    pallas_call x1, Pallas kernels, shards(): pl.pallas_call(functools.partial(kernel, sections, tiles), out_shape=(jax...  25.8 us
    unnamed x4, local copies, waits for them, and re-layouts  2.3 us

profile of v4, /device:TPU:0, one launch (start us, length us, event | category | flops | bytes accessed | tf_op | source)
XLA Modules:
  0.0 28.7 jit_solution(15620515641365708238)
XLA Ops:
  0.6 25.8 %shard_map.158 = (f32[1,128,512]{2,1,0:T(8,128)}, f32[2,16,256]{2,1,0:T(8,128)}) custom-call(f32[1,128,512]{2,1,0:T(8,128)} %state.1, bf16[1,128,512]{2,1,0:T(8,128)(2,1)} %tendency.1, bf16[1,128,512]{2,1,0:T(8,128)(2,1)} %diffusion.1, f32[1,128,128]{2,1,0:T(8,128)} %mixing.1, f32[1,128]{1,0:T(1,128)} %coupling.1, s32[1,4,512]{2,1,0:T(4,128)} %remap_index.1, ...), custom_call_target="tpu_custom_call" | custom-call | flops 700000000 | bytes 1500000 | tf_op jit(solution)/shard_map/pallas_call | solution.py:548
  26.4 0.0 copy-start
  26.4 1.7 %copy.19 = f32[1,128,512]{2,1,0:T(8,128)} copy(f32[1,128,512]{2,1,0:T(8,128)} %get-tuple-element.4) | data formatting | bytes 524288
  28.1 0.0 copy-done
  28.1 0.6 %copy.20 = f32[2,16,256]{2,1,0:T(8,128)} copy(f32[2,16,256]{2,1,0:T(8,128)S(1)} %copy-done) | data formatting | bytes 65536
Async XLA Ops:
  26.4 1.7 %copy-start = (f32[2,16,256]{2,1,0:T(8,128)S(1)}, f32[2,16,256]{2,1,0:T(8,128)}, u32[]{:S(2)}) copy-start(f32[2,16,256]{2,1,0:T(8,128)} %get-tuple-element.5) | copy-start | bytes 98308

commit v5 on v4

--- a/solution.py
+++ b/solution.py
@@ -54,10 +54,8 @@
     occ_weight,
     occ_count,
     refraction,
-    abel_matrix,
-    observed,
     out_state,
-    out_departures,
+    parts_in,
     field,
     rates,
     forcing,
@@ -73,9 +71,6 @@
     ow_v,
     oc_v,
     refr_v,
-    abel_v,
-    obs_v,
-    dep_v,
     mix_a,
     mix_b,
     pick_v,
@@ -91,7 +86,6 @@
     chosen_out,
     chosen_in,
     parts_out,
-    parts_in,
     load_sem,
     store_sem,
     pack_send,
@@ -113,7 +107,7 @@
     is_ocean = s == ocean
     right = lax.rem(t + 1, tiles)
     left = lax.rem(t + tiles - 1, tiles)
-    near = ((t, 0), (left, 1), (right, 2))
+    near = ((left, 1), (right, 2), (t, 0))
 
     loads = [
         (state.at[0], field.at[:, 0:columns]),
@@ -128,8 +122,6 @@
         (occ_weight, ow_v),
         (occ_count, oc_v),
         (refraction.at[0], refr_v),
-        (abel_matrix, abel_v),
-        (observed, obs_v),
     ]
     loads = [pltpu.make_async_copy(a, b, load_sem.at[i]) for i, (a, b) in enumerate(loads)]
     def over_tiles(body):
@@ -403,15 +395,7 @@
         parts_out[p] = part.reshape(sections, own, levels)
         for other in others():
             part_copy(p, other, s).start()
-        parts_in[p, s] = parts_out[p, s]
-
-    def depart(p):
-        for other in others():
-            part_copy(p, other, other).wait_recv()
-        total = parts_in[p, 0]
-        for a in range(1, sections):
-            total = total + parts_in[p, a]
-        dep_v[p] = obs_v[p] - dot3(total, abel_v[...])
+        pltpu.make_async_copy(parts_out.at[p, s], parts_in.at[p, s], red_recv.at[p, s]).start()
 
     def list_columns(p, carry):
         pick_v[p] = selector(p)
@@ -471,15 +455,48 @@
     lax.fori_loop(0, STEPS, gather_parts, 0)
 
     def finish(p, carry):
-        depart(p)
+        for other in others():
+            part_copy(p, other, other).wait_recv()
+        pltpu.make_async_copy(parts_out.at[p, s], parts_in.at[p, s], red_recv.at[p, s]).wait()
         for other in others():
             part_copy(p, other, s).wait_send()
         return carry
 
     lax.fori_loop(0, STEPS, finish, 0)
-    last = pltpu.make_async_copy(dep_v, out_departures, store_sem.at[1])
+    store.wait()
+
+
+CHUNKS = 4
+
+
+def departing(state, parts, abel_matrix, observed, out_state, out_departures, state_v, parts_v, abel_v, obs_v, dep_v, sem):
+    rows = state.shape[1] // CHUNKS
+    loads = [
+        pltpu.make_async_copy(parts, parts_v, sem.at[0]),
+        pltpu.make_async_copy(abel_matrix, abel_v, sem.at[1]),
+        pltpu.make_async_copy(observed, obs_v, sem.at[2]),
+    ]
+    bring, take = [], []
+    for i in range(CHUNKS):
+        at = pl.ds(i * rows, rows)
+        bring.append(pltpu.make_async_copy(state.at[:, at], state_v.at[:, at], sem.at[3 + i]))
+        take.append(pltpu.make_async_copy(state_v.at[:, at], out_state.at[:, at], sem.at[3 + CHUNKS + i]))
+    for copy in bring + loads:
+        copy.start()
+    for i in range(CHUNKS):
+        bring[i].wait()
+        take[i].start()
+    for copy in loads:
+        copy.wait()
+    for p in range(STEPS):
+        total = parts_v[p, 0]
+        for a in range(1, parts_v.shape[1]):
+            total = total + parts_v[p, a]
+        dep_v[p] = obs_v[p] - dot3(total, abel_v[...])
+    last = pltpu.make_async_copy(dep_v, out_departures, sem.at[3 + 2 * CHUNKS])
     last.start()
-    store.wait()
+    for copy in take:
+        copy.wait()
     last.wait()
 
 
@@ -497,6 +514,7 @@
     dma = pltpu.SemaphoreType.DMA
     any_spec = pl.BlockSpec(memory_space=pltpu.HBM)
     smem = pl.BlockSpec(memory_space=pltpu.SMEM)
+    args = args[:13]
     specs = [any_spec] * len(args)
     specs[7] = smem
     scratch = [
@@ -515,9 +533,6 @@
         pltpu.VMEM(occ_weight.shape, F32),
         pltpu.VMEM(occ_count.shape, jnp.int32),
         pltpu.VMEM((levels, levels), F32),
-        pltpu.VMEM(abel_matrix.shape, F32),
-        pltpu.VMEM(observed.shape, F32),
-        pltpu.VMEM(observed.shape, F32),
         pltpu.VMEM((levels, 2 * levels), BF16),
         pltpu.VMEM((levels, levels), BF16),
         pltpu.VMEM((STEPS, tiles * 8, columns), BF16),
@@ -533,9 +548,8 @@
         pltpu.VMEM((STEPS, tiles, 8, levels), F32),
         pltpu.VMEM((STEPS, tiles, 8, levels), F32),
         pltpu.VMEM((STEPS, sections, own, levels), F32),
-        pltpu.VMEM((STEPS, sections, own, levels), F32),
-        dma((14,)),
-        dma((2,)),
+        dma((12,)),
+        dma((1,)),
         dma((2,)),
         dma((2,)),
         dma((STEPS, 3, sections - 1)),
@@ -545,11 +559,11 @@
         dma((STEPS, sections)),
         dma((STEPS, sections)),
     ]
-    return pl.pallas_call(
+    middle, parts = pl.pallas_call(
         functools.partial(kernel, sections, tiles),
         out_shape=(
             jax.ShapeDtypeStruct(state.shape, F32),
-            jax.ShapeDtypeStruct((STEPS, own, heights), F32),
+            jax.ShapeDtypeStruct((STEPS, sections, own, levels), F32),
         ),
         in_specs=specs,
         out_specs=(any_spec, any_spec),
@@ -559,6 +573,22 @@
         ),
         cost_estimate=pl.CostEstimate(flops=700_000_000, bytes_accessed=1_500_000, transcendentals=0),
     )(*args)
+    return pl.pallas_call(
+        departing,
+        out_shape=(jax.ShapeDtypeStruct(state.shape, F32), jax.ShapeDtypeStruct((STEPS, own, heights), F32)),
+        in_specs=[any_spec] * 4,
+        out_specs=(any_spec, any_spec),
+        scratch_shapes=[
+            pltpu.VMEM(state.shape, F32),
+            pltpu.VMEM(parts.shape, F32),
+            pltpu.VMEM(abel_matrix.shape, F32),
+            pltpu.VMEM(observed.shape, F32),
+            pltpu.VMEM(observed.shape, F32),
+            dma((4 + 2 * CHUNKS,)),
+        ],
+        compiler_params=pltpu.CompilerParams(vmem_limit_bytes=64 * 1024 * 1024 - 64 * 1024),
+        cost_estimate=pl.CostEstimate(flops=10_000_000, bytes_accessed=800_000, transcendentals=0),
+    )(middle, parts, abel_matrix, observed)
 
 
 def solution(mesh):

time: 28.9 us -> 27.9 us (0.965)
  local copies, waits for them, and re-layouts: 2.3 us -> 0 us
  Pallas kernels: 25.8 us -> 27.1 us
    unnamed x4 -> x0, local copies, waits for them, and re-layouts: 2.3 us -> none
    pallas_call x0 -> x1, Pallas kernels: none -> 1.96 us  [shards(): pl.pallas_call(departing, out_shape=(jax.ShapeDtypeStruct(state.shape, F3...]
    pallas_call x1, Pallas kernels: 25.8 us -> 25.1 us  [shards(): pl.pallas_call(functools.partial(kernel, sections, tiles), out_shape=(jax...]
where the time goes in v5:
time: 27.9 us; the launch traced here: 27.7 us
  Pallas kernels  27.1 us (97%)
  between operations  0.64 us (2%)
    pallas_call x1, Pallas kernels, shards(): pl.pallas_call(functools.partial(kernel, sections, tiles), out_shape=(jax...  25.1 us
    pallas_call x1, Pallas kernels, shards(): pl.pallas_call(departing, out_shape=(jax.ShapeDtypeStruct(state.shape, F3...  1.96 us

profile of v5, /device:TPU:0, one launch (start us, length us, event | category | flops | bytes accessed | tf_op | source)
XLA Modules:
  0.0 27.7 jit_solution(7459836678602216767)
XLA Ops:
  0.6 25.1 %shard_map.158 = (f32[1,128,512]{2,1,0:T(8,128)}, f32[2,4,16,128]{3,2,1,0:T(8,128)}) custom-call(f32[1,128,512]{2,1,0:T(8,128)} %state.1, bf16[1,128,512]{2,1,0:T(8,128)(2,1)} %tendency.1, bf16[1,128,512]{2,1,0:T(8,128)(2,1)} %diffusion.1, f32[1,128,128]{2,1,0:T(8,128)} %mixing.1, f32[1,128]{1,0:T(1,128)} %coupling.1, s32[1,4,512]{2,1,0:T(4,128)} %remap_index.1, ...), custom_call_target="tpu_custom_call" | custom-call | flops 700000000 | bytes 1500000 | tf_op jit(solution)/shard_map/pallas_call | solution.py:562
  25.7 2.0 %shard_map.159 = (f32[1,128,512]{2,1,0:T(8,128)}, f32[2,16,256]{2,1,0:T(8,128)}) custom-call(f32[1,128,512]{2,1,0:T(8,128)} %get-tuple-element.4.state, f32[2,4,16,128]{3,2,1,0:T(8,128)} %get-tuple-element.5.parts, f32[128,256]{1,0:T(8,128)} %abel_matrix.1, f32[2,16,256]{2,1,0:T(8,128)} %observed.1), custom_call_target="tpu_custom_call" | custom-call | flops 10000000 | bytes 800000 | tf_op jit(solution)/shard_map/pallas_call | solution.py:576

commit v6 on v5

--- a/solution.py
+++ b/solution.py
@@ -56,6 +56,8 @@
     refraction,
     out_state,
     parts_in,
+    cols_in,
+    rows_in,
     field,
     rates,
     forcing,
@@ -74,7 +76,6 @@
     mix_a,
     mix_b,
     pick_v,
-    occ_v,
     gain,
     position,
     weight,
@@ -86,6 +87,7 @@
     chosen_out,
     chosen_in,
     parts_out,
+    rows_out,
     load_sem,
     store_sem,
     pack_send,
@@ -96,6 +98,10 @@
     col_recv,
     red_send,
     red_recv,
+    last_send,
+    last_recv,
+    row_send,
+    row_recv,
 ):
     levels, columns = tend_v.shape
     ext = field.shape[1]
@@ -136,20 +142,13 @@
     def greet(sec, tile):
         pl.semaphore_signal(barrier, inc=1, device_id=(sec, tile), device_id_type=MESH)
 
-    over_tiles(lambda other: greet(s, other))
-    for d in range(1, sections):
-        greet(lax.rem(s + d, sections), t)
-
-    @pl.when(is_ocean)
-    def _():
-        for a in range(ocean):
-            greet(a, left)
-            greet(a, right)
-
-    @pl.when(jnp.logical_not(is_ocean))
-    def _():
-        greet(ocean, left)
-        greet(ocean, right)
+    def beyond(body):
+        for q in range(sections):
+            over_tiles(lambda other: body(lax.rem(s + q, sections), other))
+        for d in range(1, sections):
+            body(lax.rem(s + d, sections), t)
+
+    beyond(greet)
 
     for load in loads:
         load.start()
@@ -180,8 +179,7 @@
     pack(0, 0, 0)
     pack(1, tail, HALO)
 
-    meet = (tiles - 1) + (sections - 1) + jnp.where(is_ocean, 2 * ocean, 2)
-    pl.semaphore_wait(barrier, meet)
+    pl.semaphore_wait(barrier, sections * tiles - 1)
 
     def pack_copy(slot, tile):
         return pltpu.make_async_remote_copy(
@@ -365,14 +363,48 @@
             device_id_type=MESH,
         )
 
+    def last_copy(sec, other, from_sec, from_tile):
+        return pltpu.make_async_remote_copy(
+            src_ref=chosen_out.at[STEPS - 1, other, 0:cap],
+            dst_ref=cols_in.at[from_sec, from_tile, 0:cap],
+            send_sem=last_send.at[sec, other],
+            recv_sem=last_recv.at[from_sec, from_tile],
+            device_id=(sec, other),
+            device_id_type=MESH,
+        )
+
+    own_columns = pltpu.make_async_copy(
+        chosen_out.at[STEPS - 1, t, 0:cap], cols_in.at[s, t, 0:cap], last_recv.at[s, t]
+    )
+
+    def row_copy(sec, source):
+        return pltpu.make_async_remote_copy(
+            src_ref=rows_out.at[sec],
+            dst_ref=rows_in.at[source],
+            send_sem=row_send.at[sec],
+            recv_sem=row_recv.at[source],
+            device_id=(sec, t),
+            device_id_type=MESH,
+        )
+
+    own_rows = pltpu.make_async_copy(rows_out.at[s], rows_in.at[s], row_recv.at[s])
+
     def send_columns(p):
         pick = pick_v[p]
         fh, fl = split(field[:, 0:columns])
         taken = mm(pick, fh, NT) + mm(pick, fl, NT)
         projected = dot3(taken, refr_v[...]).reshape(tiles, 8, levels)
         chosen_out[p] = projected
-        over_tiles(lambda other: column_copy(p, other, t).start())
-        chosen_in[p, t] = chosen_out[p, t]
+
+        @pl.when(p < STEPS - 1)
+        def _():
+            over_tiles(lambda other: column_copy(p, other, t).start())
+            chosen_in[p, t] = chosen_out[p, t]
+
+        @pl.when(p == STEPS - 1)
+        def _():
+            beyond(lambda sec, other: last_copy(sec, other, s, t).start())
+            own_columns.start()
 
     own = parts_out.shape[2]
 
@@ -433,26 +465,22 @@
 
     lax.fori_loop(0, STEPS, period, 0)
 
-    def weigh(p, carry):
-        occ_v[p] = occultation_weights(p)
-        return carry
-
-    lax.fori_loop(0, STEPS, weigh, 0)
-
     def gather_parts(p, carry):
-        send_parts(p, occ_v[p])
-
-        @pl.when(p == 0)
-        def _():
-            for copy in packs:
-                copy.wait_send()
-            for q in range(STEPS):
-                surf_each(q, lambda copy: copy.wait_send())
-
+        send_parts(p, occultation_weights(p))
         over_tiles(lambda other: column_copy(p, other, t).wait_send())
         return carry
 
-    lax.fori_loop(0, STEPS, gather_parts, 0)
+    lax.fori_loop(0, STEPS - 1, gather_parts, 0)
+    rows_out[...] = occultation_weights(STEPS - 1).T.reshape(rows_out.shape)
+    for other in others():
+        row_copy(other, s).start()
+    own_rows.start()
+
+    for copy in packs:
+        copy.wait_send()
+    for q in range(STEPS):
+        surf_each(q, lambda copy: copy.wait_send())
+    store.wait()
 
     def finish(p, carry):
         for other in others():
@@ -462,38 +490,73 @@
             part_copy(p, other, s).wait_send()
         return carry
 
-    lax.fori_loop(0, STEPS, finish, 0)
-    store.wait()
+    lax.fori_loop(0, STEPS - 1, finish, 0)
+    beyond(lambda sec, other: last_copy(sec, other, s, t).wait_send())
+    own_columns.wait()
+    for other in others():
+        row_copy(other, s).wait_send()
+    beyond(lambda sec, other: last_copy(sec, other, sec, other).wait_recv())
+    for other in others():
+        row_copy(other, other).wait_recv()
+    own_rows.wait()
 
 
 CHUNKS = 4
 
 
-def departing(state, parts, abel_matrix, observed, out_state, out_departures, state_v, parts_v, abel_v, obs_v, dep_v, sem):
+def departing(
+    cap,
+    state,
+    parts,
+    cols,
+    weights,
+    abel_matrix,
+    observed,
+    out_state,
+    out_departures,
+    state_v,
+    parts_v,
+    cols_v,
+    weights_v,
+    abel_v,
+    obs_v,
+    dep_v,
+    sem,
+):
     rows = state.shape[1] // CHUNKS
     loads = [
-        pltpu.make_async_copy(parts, parts_v, sem.at[0]),
-        pltpu.make_async_copy(abel_matrix, abel_v, sem.at[1]),
-        pltpu.make_async_copy(observed, obs_v, sem.at[2]),
+        pltpu.make_async_copy(cols, cols_v, sem.at[0]),
+        pltpu.make_async_copy(weights, weights_v, sem.at[1]),
+        pltpu.make_async_copy(parts, parts_v, sem.at[2]),
+        pltpu.make_async_copy(abel_matrix, abel_v, sem.at[3]),
+        pltpu.make_async_copy(observed, obs_v, sem.at[4]),
     ]
     bring, take = [], []
     for i in range(CHUNKS):
         at = pl.ds(i * rows, rows)
-        bring.append(pltpu.make_async_copy(state.at[:, at], state_v.at[:, at], sem.at[3 + i]))
-        take.append(pltpu.make_async_copy(state_v.at[:, at], out_state.at[:, at], sem.at[3 + CHUNKS + i]))
-    for copy in bring + loads:
+        bring.append(pltpu.make_async_copy(state.at[:, at], state_v.at[:, at], sem.at[5 + i]))
+        take.append(pltpu.make_async_copy(state_v.at[:, at], out_state.at[:, at], sem.at[5 + CHUNKS + i]))
+    for copy in loads + bring:
         copy.start()
     for i in range(CHUNKS):
         bring[i].wait()
         take[i].start()
     for copy in loads:
         copy.wait()
+    sections, _, columns = weights_v.shape
+    levels = cols_v.shape[3]
+    sent = (lax.broadcasted_iota(jnp.int32, (columns, levels), 0) & 7) < cap
+    totals = []
+    for p in range(STEPS - 1):
+        totals.append(parts_v[p, 0])
+        for a in range(1, sections):
+            totals[p] = totals[p] + parts_v[p, a]
+    for a in range(sections):
+        term = dot3(weights_v[a], jnp.where(sent, cols_v[a].reshape(columns, levels), 0.0))
+        totals.append(term) if a == 0 else totals.append(totals.pop() + term)
     for p in range(STEPS):
-        total = parts_v[p, 0]
-        for a in range(1, parts_v.shape[1]):
-            total = total + parts_v[p, a]
-        dep_v[p] = obs_v[p] - dot3(total, abel_v[...])
-    last = pltpu.make_async_copy(dep_v, out_departures, sem.at[3 + 2 * CHUNKS])
+        dep_v[p] = obs_v[p] - dot3(totals[p], abel_v[...])
+    last = pltpu.make_async_copy(dep_v, out_departures, sem.at[5 + 2 * CHUNKS])
     last.start()
     for copy in take:
         copy.wait()
@@ -536,7 +599,6 @@
         pltpu.VMEM((levels, 2 * levels), BF16),
         pltpu.VMEM((levels, levels), BF16),
         pltpu.VMEM((STEPS, tiles * 8, columns), BF16),
-        pltpu.VMEM((STEPS, tiles * 8, occ_slot.shape[3]), F32),
         pltpu.VMEM((levels, LANES), F32),
         pltpu.VMEM((slots, LANES), jnp.int32),
         pltpu.VMEM((slots, LANES), F32),
@@ -547,7 +609,8 @@
         pltpu.VMEM((2, PACK, LANES), F32),
         pltpu.VMEM((STEPS, tiles, 8, levels), F32),
         pltpu.VMEM((STEPS, tiles, 8, levels), F32),
-        pltpu.VMEM((STEPS, sections, own, levels), F32),
+        pltpu.VMEM((STEPS - 1, sections, own, levels), F32),
+        pltpu.VMEM((sections, own, tiles * 8), F32),
         dma((12,)),
         dma((1,)),
         dma((2,)),
@@ -558,15 +621,21 @@
         dma((STEPS, tiles)),
         dma((STEPS, sections)),
         dma((STEPS, sections)),
+        dma((sections, tiles)),
+        dma((sections, tiles)),
+        dma((sections,)),
+        dma((sections,)),
     ]
-    middle, parts = pl.pallas_call(
+    middle, parts, cols, weights = pl.pallas_call(
         functools.partial(kernel, sections, tiles),
         out_shape=(
             jax.ShapeDtypeStruct(state.shape, F32),
-            jax.ShapeDtypeStruct((STEPS, sections, own, levels), F32),
+            jax.ShapeDtypeStruct((STEPS - 1, sections, own, levels), F32),
+            jax.ShapeDtypeStruct((sections, tiles, 8, levels), F32),
+            jax.ShapeDtypeStruct((sections, own, tiles * 8), F32),
         ),
         in_specs=specs,
-        out_specs=(any_spec, any_spec),
+        out_specs=(any_spec,) * 4,
         scratch_shapes=scratch,
         compiler_params=pltpu.CompilerParams(
             collective_id=0, has_side_effects=True, vmem_limit_bytes=64 * 1024 * 1024 - 64 * 1024
@@ -574,21 +643,23 @@
         cost_estimate=pl.CostEstimate(flops=700_000_000, bytes_accessed=1_500_000, transcendentals=0),
     )(*args)
     return pl.pallas_call(
-        departing,
+        functools.partial(departing, send_cols.shape[3]),
         out_shape=(jax.ShapeDtypeStruct(state.shape, F32), jax.ShapeDtypeStruct((STEPS, own, heights), F32)),
-        in_specs=[any_spec] * 4,
+        in_specs=[any_spec] * 6,
         out_specs=(any_spec, any_spec),
         scratch_shapes=[
             pltpu.VMEM(state.shape, F32),
             pltpu.VMEM(parts.shape, F32),
+            pltpu.VMEM(cols.shape, F32),
+            pltpu.VMEM(weights.shape, F32),
             pltpu.VMEM(abel_matrix.shape, F32),
             pltpu.VMEM(observed.shape, F32),
             pltpu.VMEM(observed.shape, F32),
-            dma((4 + 2 * CHUNKS,)),
+            dma((6 + 2 * CHUNKS,)),
         ],
         compiler_params=pltpu.CompilerParams(vmem_limit_bytes=64 * 1024 * 1024 - 64 * 1024),
         cost_estimate=pl.CostEstimate(flops=10_000_000, bytes_accessed=800_000, transcendentals=0),
-    )(middle, parts, abel_matrix, observed)
+    )(middle, parts, cols, weights, abel_matrix, observed)
 
 
 def solution(mesh):

time: 27.9 us -> 27.8 us (level)
    pallas_call x1, Pallas kernels: 25.1 us -> 24.7 us  [shards(): pl.pallas_call(functools.partial(kernel, sections, tiles), out_shape=(jax...]
where the time goes in v6:
time: 27.8 us; the launch traced here: 27.6 us
  Pallas kernels  27 us (97%)
  between operations  0.64 us (2%)
    pallas_call x1, Pallas kernels, shards(): pl.pallas_call(functools.partial(kernel, sections, tiles), out_shape=(jax...  24.7 us
    pallas_call x1, Pallas kernels, shards(): pl.pallas_call(functools.partial(departing, send_cols.shape[3]), out_shap...  2.24 us

profile of v6, /device:TPU:0, one launch (start us, length us, event | category | flops | bytes accessed | tf_op | source)
XLA Modules:
  0.0 27.6 jit_solution(16264384728570535936)
XLA Ops:
  0.6 24.7 %shard_map.158 = (f32[1,128,512]{2,1,0:T(8,128)}, f32[1,4,16,128]{3,2,1,0:T(8,128)}, f32[4,8,8,128]{3,2,1,0:T(8,128)}, f32[4,16,64]{2,1,0:T(8,128)}) custom-call(f32[1,128,512]{2,1,0:T(8,128)} %state.1, bf16[1,128,512]{2,1,0:T(8,128)(2,1)} %tendency.1, bf16[1,128,512]{2,1,0:T(8,128)(2,1)} %diffusion.1, f32[1,128,128]{2,1,0:T(8,128)} %mixing.1, ...), custom_call_target="tpu_custom_call" | custom-call | flops 700000000 | bytes 1500000 | tf_op jit(solution)/shard_map/pallas_call | solution.py:629
  25.4 2.2 %shard_map.159 = (f32[1,128,512]{2,1,0:T(8,128)}, f32[2,16,256]{2,1,0:T(8,128)}) custom-call(f32[1,128,512]{2,1,0:T(8,128)} %get-tuple-element.6.state, f32[1,4,16,128]{3,2,1,0:T(8,128)} %get-tuple-element.7.parts, f32[4,8,8,128]{3,2,1,0:T(8,128)} %get-tuple-element.8.cols, f32[4,16,64]{2,1,0:T(8,128)} %get-tuple-element.9.weights, f32[128,256]{1,0:T(8,128)} %abel_matrix.1, ...), custom_call_target="tpu_custom_call" | custom-call | flops 10000000 | bytes 800000 | tf_op jit(solution)/shard_map/pallas_call | solution.py:645

commit v7 on v6

--- a/solution.py
+++ b/solution.py
@@ -88,6 +88,7 @@
     chosen_in,
     parts_out,
     rows_out,
+    spare,
     load_sem,
     store_sem,
     pack_send,
@@ -130,6 +131,12 @@
         (refraction.at[0], refr_v),
     ]
     loads = [pltpu.make_async_copy(a, b, load_sem.at[i]) for i, (a, b) in enumerate(loads)]
+    for load in loads[:5]:
+        load.start()
+
+    def drain(ref, sem):
+        pltpu.make_async_copy(ref, ref, sem).wait()
+
     def over_tiles(body):
         if tiles <= 8:
             for d in range(1, tiles):
@@ -150,7 +157,7 @@
 
     beyond(greet)
 
-    for load in loads:
+    for load in loads[5:]:
         load.start()
 
     lane = lax.broadcasted_iota(jnp.int32, (levels, LANES), 1)
@@ -195,11 +202,21 @@
         return pltpu.make_async_remote_copy(
             src_ref=surf.at[p],
             dst_ref=tab.at[p, d, a],
-            send_sem=surf_send.at[p, d, mark],
-            recv_sem=surf_recv.at[p, d, a],
+            send_sem=surf_send.at[p, mark],
+            recv_sem=surf_recv.at[p, a],
             device_id=(sec, tile),
             device_id_type=MESH,
         )
+
+    def surf_sent(p):
+        @pl.when(is_ocean)
+        def _():
+            for a in range(ocean):
+                drain(tab.at[p, :, a], surf_send.at[p, a])
+
+        @pl.when(jnp.logical_not(is_ocean))
+        def _():
+            drain(tab.at[p, :, 0], surf_send.at[p, 0])
 
     def surf_each(p, act):
         @pl.when(is_ocean)
@@ -288,15 +305,7 @@
         outer = lax.shift_right_logical(pos, 7)
 
         def look(a):
-            for d in range(3):
-                pltpu.make_async_remote_copy(
-                    src_ref=surf.at[p],
-                    dst_ref=tab.at[p, d, a],
-                    send_sem=surf_send.at[p, d, 0],
-                    recv_sem=surf_recv.at[p, d, a],
-                    device_id=(s, right),
-                    device_id_type=MESH,
-                ).wait_recv()
+            drain(tab.at[p, :, a], surf_recv.at[p, a])
             found = picked[...]
             for b in range(blocks):
                 at = slice(b * LANES, (b + 1) * LANES)
@@ -357,8 +366,8 @@
         return pltpu.make_async_remote_copy(
             src_ref=chosen_out.at[p, other],
             dst_ref=chosen_in.at[p, source],
-            send_sem=col_send.at[p, other],
-            recv_sem=col_recv.at[p, source],
+            send_sem=col_send.at[p],
+            recv_sem=col_recv.at[p],
             device_id=(s, other),
             device_id_type=MESH,
         )
@@ -367,27 +376,27 @@
         return pltpu.make_async_remote_copy(
             src_ref=chosen_out.at[STEPS - 1, other, 0:cap],
             dst_ref=cols_in.at[from_sec, from_tile, 0:cap],
-            send_sem=last_send.at[sec, other],
-            recv_sem=last_recv.at[from_sec, from_tile],
+            send_sem=last_send.at[0],
+            recv_sem=last_recv.at[0],
             device_id=(sec, other),
             device_id_type=MESH,
         )
 
     own_columns = pltpu.make_async_copy(
-        chosen_out.at[STEPS - 1, t, 0:cap], cols_in.at[s, t, 0:cap], last_recv.at[s, t]
+        chosen_out.at[STEPS - 1, t, 0:cap], cols_in.at[s, t, 0:cap], last_recv.at[0]
     )
 
     def row_copy(sec, source):
         return pltpu.make_async_remote_copy(
             src_ref=rows_out.at[sec],
             dst_ref=rows_in.at[source],
-            send_sem=row_send.at[sec],
-            recv_sem=row_recv.at[source],
+            send_sem=row_send.at[0],
+            recv_sem=row_recv.at[0],
             device_id=(sec, t),
             device_id_type=MESH,
         )
 
-    own_rows = pltpu.make_async_copy(rows_out.at[s], rows_in.at[s], row_recv.at[s])
+    own_rows = pltpu.make_async_copy(rows_out.at[s], rows_in.at[s], row_recv.at[0])
 
     def send_columns(p):
         pick = pick_v[p]
@@ -399,7 +408,7 @@
         @pl.when(p < STEPS - 1)
         def _():
             over_tiles(lambda other: column_copy(p, other, t).start())
-            chosen_in[p, t] = chosen_out[p, t]
+            pltpu.make_async_copy(chosen_out.at[p, t], chosen_in.at[p, t], col_recv.at[p]).start()
 
         @pl.when(p == STEPS - 1)
         def _():
@@ -412,8 +421,8 @@
         return pltpu.make_async_remote_copy(
             src_ref=parts_out.at[p, other],
             dst_ref=parts_in.at[p, source],
-            send_sem=red_send.at[p, other],
-            recv_sem=red_recv.at[p, source],
+            send_sem=red_send.at[p],
+            recv_sem=red_recv.at[p],
             device_id=(other, t),
             device_id_type=MESH,
         )
@@ -422,12 +431,12 @@
         return [lax.rem(s + d, sections) for d in range(1, sections)]
 
     def send_parts(p, w):
-        over_tiles(lambda other: column_copy(p, other, other).wait_recv())
+        drain(chosen_in.at[p], col_recv.at[p])
         part = dot3(w, chosen_in[p].reshape(rows, levels), TN)
         parts_out[p] = part.reshape(sections, own, levels)
         for other in others():
             part_copy(p, other, s).start()
-        pltpu.make_async_copy(parts_out.at[p, s], parts_in.at[p, s], red_recv.at[p, s]).start()
+        pltpu.make_async_copy(parts_out.at[p, s], parts_in.at[p, s], red_recv.at[p]).start()
 
     def list_columns(p, carry):
         pick_v[p] = selector(p)
@@ -467,7 +476,7 @@
 
     def gather_parts(p, carry):
         send_parts(p, occultation_weights(p))
-        over_tiles(lambda other: column_copy(p, other, t).wait_send())
+        drain(chosen_out.at[p, 0 : tiles - 1], col_send.at[p])
         return carry
 
     lax.fori_loop(0, STEPS - 1, gather_parts, 0)
@@ -479,26 +488,16 @@
     for copy in packs:
         copy.wait_send()
     for q in range(STEPS):
-        surf_each(q, lambda copy: copy.wait_send())
+        surf_sent(q)
     store.wait()
 
-    def finish(p, carry):
-        for other in others():
-            part_copy(p, other, other).wait_recv()
-        pltpu.make_async_copy(parts_out.at[p, s], parts_in.at[p, s], red_recv.at[p, s]).wait()
-        for other in others():
-            part_copy(p, other, s).wait_send()
-        return carry
-
-    lax.fori_loop(0, STEPS - 1, finish, 0)
-    beyond(lambda sec, other: last_copy(sec, other, s, t).wait_send())
-    own_columns.wait()
-    for other in others():
-        row_copy(other, s).wait_send()
-    beyond(lambda sec, other: last_copy(sec, other, sec, other).wait_recv())
-    for other in others():
-        row_copy(other, other).wait_recv()
-    own_rows.wait()
+    drain(spare, last_send.at[0])
+    drain(rows_out.at[0 : sections - 1], row_send.at[0])
+    for p in range(STEPS - 1):
+        drain(parts_out.at[p, 0 : sections - 1], red_send.at[p])
+        drain(parts_in.at[p], red_recv.at[p])
+    drain(rows_in, row_recv.at[0])
+    drain(cols_in.at[:, :, 0:cap], last_recv.at[0])
 
 
 CHUNKS = 4
@@ -611,20 +610,21 @@
         pltpu.VMEM((STEPS, tiles, 8, levels), F32),
         pltpu.VMEM((STEPS - 1, sections, own, levels), F32),
         pltpu.VMEM((sections, own, tiles * 8), F32),
+        pltpu.VMEM((sections * tiles - 1, send_cols.shape[3], levels), F32),
         dma((12,)),
         dma((1,)),
         dma((2,)),
         dma((2,)),
-        dma((STEPS, 3, sections - 1)),
-        dma((STEPS, 3, sections - 1)),
-        dma((STEPS, tiles)),
-        dma((STEPS, tiles)),
-        dma((STEPS, sections)),
-        dma((STEPS, sections)),
-        dma((sections, tiles)),
-        dma((sections, tiles)),
-        dma((sections,)),
-        dma((sections,)),
+        dma((STEPS, sections - 1)),
+        dma((STEPS, sections - 1)),
+        dma((STEPS,)),
+        dma((STEPS,)),
+        dma((STEPS,)),
+        dma((STEPS,)),
+        dma((1,)),
+        dma((1,)),
+        dma((1,)),
+        dma((1,)),
     ]
     middle, parts, cols, weights = pl.pallas_call(
         functools.partial(kernel, sections, tiles),

time: 27.8 us -> 26.5 us (0.953)
  Pallas kernels: 27 us -> 25.7 us
    pallas_call x1, Pallas kernels: 24.7 us -> 23.5 us  [shards(): pl.pallas_call(functools.partial(kernel, sections, tiles), out_shape=(jax...]
where the time goes in v7:
time: 26.5 us; the launch traced here: 26.4 us
  Pallas kernels  25.7 us (97%)
  between operations  0.64 us (2%)
    pallas_call x1, Pallas kernels, shards(): pl.pallas_call(functools.partial(kernel, sections, tiles), out_shape=(jax...  23.5 us
    pallas_call x1, Pallas kernels, shards(): pl.pallas_call(functools.partial(departing, send_cols.shape[3]), out_shap...  2.24 us

profile of v7, /device:TPU:0, one launch (start us, length us, event | category | flops | bytes accessed | tf_op | source)
XLA Modules:
  0.0 26.4 jit_solution(9452376230800444866)
XLA Ops:
  0.6 23.5 %shard_map.158 = (f32[1,128,512]{2,1,0:T(8,128)}, f32[1,4,16,128]{3,2,1,0:T(8,128)}, f32[4,8,8,128]{3,2,1,0:T(8,128)}, f32[4,16,64]{2,1,0:T(8,128)}) custom-call(f32[1,128,512]{2,1,0:T(8,128)} %state.1, bf16[1,128,512]{2,1,0:T(8,128)(2,1)} %tendency.1, bf16[1,128,512]{2,1,0:T(8,128)(2,1)} %diffusion.1, f32[1,128,128]{2,1,0:T(8,128)} %mixing.1, ...), custom_call_target="tpu_custom_call" | custom-call | flops 700000000 | bytes 1500000 | tf_op jit(solution)/shard_map/pallas_call | solution.py:629
  24.1 2.2 %shard_map.159 = (f32[1,128,512]{2,1,0:T(8,128)}, f32[2,16,256]{2,1,0:T(8,128)}) custom-call(f32[1,128,512]{2,1,0:T(8,128)} %get-tuple-element.6.state, f32[1,4,16,128]{3,2,1,0:T(8,128)} %get-tuple-element.7.parts, f32[4,8,8,128]{3,2,1,0:T(8,128)} %get-tuple-element.8.cols, f32[4,16,64]{2,1,0:T(8,128)} %get-tuple-element.9.weights, f32[128,256]{1,0:T(8,128)} %abel_matrix.1, ...), custom_call_target="tpu_custom_call" | custom-call | flops 10000000 | bytes 800000 | tf_op jit(solution)/shard_map/pallas_call | solution.py:645

commit v8 on v7

--- a/solution.py
+++ b/solution.py
@@ -73,8 +73,7 @@
     ow_v,
     oc_v,
     refr_v,
-    mix_a,
-    mix_b,
+    mix,
     pick_v,
     gain,
     position,
@@ -238,9 +237,10 @@
     for load in loads[5:]:
         load.wait()
     mh, ml = split(mix_v[...])
-    mix_a[:, 0:levels] = mh
-    mix_a[:, levels : 2 * levels] = mh
-    mix_b[...] = ml
+    mix[0:levels, 0:levels] = mh
+    mix[0:levels, levels : 2 * levels] = mh
+    mix[levels : 2 * levels, 0:levels] = ml
+    mix[levels : 2 * levels, levels : 2 * levels] = jnp.zeros_like(ml)
     gain[...] = jnp.broadcast_to(coup_v[...], (LANES, levels)).T
     rates[:, 0:columns] = diff_v[...].astype(F32)
     forcing[:, 0:columns] = tend_v[...].astype(F32)
@@ -293,11 +293,14 @@
         around = pltpu.roll(f, 1, 1) + pltpu.roll(f, ext - 1, 1)
         spread = f + rates[...] * (around - 2.0 * f)
         xh, xl = split(spread)
-        return jnp.concatenate([xh, xl], axis=0), xh
+        return jnp.concatenate([xh, xl], axis=0)
+
+    def mixed(halves):
+        both = mm(mix[...], halves, NN)
+        return both[0:levels] + both[levels : 2 * levels]
 
     def mixed_spread():
-        xx, xh = spread_halves()
-        return mm(mix_a[...], xx, NN) + mm(mix_b[...], xh, NN)
+        return mixed(spread_halves())
 
     def boundary_of(p):
         pos = position[...]
@@ -349,17 +352,19 @@
             return carry
 
         lax.fori_loop(0, SUBS - 2, substep, 0)
-        xx, xh = spread_halves()
+        halves = spread_halves()
 
         @pl.when(p < STEPS - 1)
         def _():
             low = slice(levels - 8, levels)
-            row = mm(mix_a[low, :], xx, NN) + mm(mix_b[low, :], xh, NN) + drive[low, :]
+            ends = jnp.concatenate([mix[levels - 16 : levels, :], mix[2 * levels - 16 : 2 * levels, :]], axis=0)
+            both = mm(ends, halves, NN)
+            row = both[8:16] + both[24:32] + drive[low, :]
             row = jnp.where(live, row, field[low, :])
             surf[p + 1] = row[7:8, 0:columns]
             surf_each(p + 1, lambda copy: copy.start())
 
-        product = mm(mix_a[...], xx, NN) + mm(mix_b[...], xh, NN)
+        product = mixed(halves)
         field[...] = jnp.where(live, product + drive[...], field[...])
 
     def column_copy(p, other, source):
@@ -595,8 +600,7 @@
         pltpu.VMEM(occ_weight.shape, F32),
         pltpu.VMEM(occ_count.shape, jnp.int32),
         pltpu.VMEM((levels, levels), F32),
-        pltpu.VMEM((levels, 2 * levels), BF16),
-        pltpu.VMEM((levels, levels), BF16),
+        pltpu.VMEM((2 * levels, 2 * levels), BF16),
         pltpu.VMEM((STEPS, tiles * 8, columns), BF16),
         pltpu.VMEM((levels, LANES), F32),
         pltpu.VMEM((slots, LANES), jnp.int32),

time: 26.5 us -> 26.5 us (level)
  no operation moved by 1% of the time
where the time goes in v8:
time: 26.5 us; the launch traced here: 26.3 us
  Pallas kernels  25.7 us (97%)
  between operations  0.64 us (2%)
    pallas_call x1, Pallas kernels, shards(): pl.pallas_call(functools.partial(kernel, sections, tiles), out_shape=(jax...  23.4 us
    pallas_call x1, Pallas kernels, shards(): pl.pallas_call(functools.partial(departing, send_cols.shape[3]), out_shap...  2.24 us

profile of v8, /device:TPU:0, one launch (start us, length us, event | category | flops | bytes accessed | tf_op | source)
XLA Modules:
  0.0 26.3 jit_solution(6847557301582943316)
XLA Ops:
  0.6 23.4 %shard_map.158 = (f32[1,128,512]{2,1,0:T(8,128)}, f32[1,4,16,128]{3,2,1,0:T(8,128)}, f32[4,8,8,128]{3,2,1,0:T(8,128)}, f32[4,16,64]{2,1,0:T(8,128)}) custom-call(f32[1,128,512]{2,1,0:T(8,128)} %state.1, bf16[1,128,512]{2,1,0:T(8,128)(2,1)} %tendency.1, bf16[1,128,512]{2,1,0:T(8,128)(2,1)} %diffusion.1, f32[1,128,128]{2,1,0:T(8,128)} %mixing.1, ...), custom_call_target="tpu_custom_call" | custom-call | flops 700000000 | bytes 1500000 | tf_op jit(solution)/shard_map/pallas_call | solution.py:633
  24.1 2.2 %shard_map.159 = (f32[1,128,512]{2,1,0:T(8,128)}, f32[2,16,256]{2,1,0:T(8,128)}) custom-call(f32[1,128,512]{2,1,0:T(8,128)} %get-tuple-element.6.state, f32[1,4,16,128]{3,2,1,0:T(8,128)} %get-tuple-element.7.parts, f32[4,8,8,128]{3,2,1,0:T(8,128)} %get-tuple-element.8.cols, f32[4,16,64]{2,1,0:T(8,128)} %get-tuple-element.9.weights, f32[128,256]{1,0:T(8,128)} %abel_matrix.1, ...), custom_call_target="tpu_custom_call" | custom-call | flops 10000000 | bytes 800000 | tf_op jit(solution)/shard_map/pallas_call | solution.py:649

commit v9 on v8

--- a/solution.py
+++ b/solution.py
@@ -261,14 +261,9 @@
     def selector(p):
         which = lax.broadcasted_iota(jnp.int32, (rows, tiles), 0)
         owner = lax.broadcasted_iota(jnp.int32, (rows, tiles), 1)
-        expand = jnp.where(lax.shift_right_logical(which, 3) == owner, 1.0, 0.0)
-        listed = lax.dot_general(
-            expand,
-            cols_v[p, 0, 0].astype(F32),
-            (NT, ((), ())),
-            precision=lax.Precision.HIGHEST,
-            preferred_element_type=F32,
-        )
+        expand = jnp.where(lax.shift_right_logical(which, 3) == owner, 1.0, 0.0).astype(BF16)
+        high, low = split(cols_v[p, 0, 0].astype(F32))
+        listed = mm(expand, high, NT) + mm(expand, low, NT)
         r = lax.broadcasted_iota(jnp.int32, (rows, cap), 0)
         c = lax.broadcasted_iota(jnp.int32, (rows, cap), 1)
         column = jnp.sum(jnp.where((r & 7) == c, listed, 0.0), axis=1, keepdims=True)

time: 26.5 us -> 26.5 us (level)
  no operation moved by 1% of the time
where the time goes in v9:
time: 26.5 us; the launch traced here: 26.3 us
  Pallas kernels  25.7 us (97%)
  between operations  0.64 us (2%)
    pallas_call x1, Pallas kernels, shards(): pl.pallas_call(functools.partial(kernel, sections, tiles), out_shape=(jax...  23.4 us
    pallas_call x1, Pallas kernels, shards(): pl.pallas_call(functools.partial(departing, send_cols.shape[3]), out_shap...  2.24 us

profile of v9, /device:TPU:0, one launch (start us, length us, event | category | flops | bytes accessed | tf_op | source)
XLA Modules:
  0.0 26.3 jit_solution(2320853605203663796)
XLA Ops:
  0.6 23.4 %shard_map.158 = (f32[1,128,512]{2,1,0:T(8,128)}, f32[1,4,16,128]{3,2,1,0:T(8,128)}, f32[4,8,8,128]{3,2,1,0:T(8,128)}, f32[4,16,64]{2,1,0:T(8,128)}) custom-call(f32[1,128,512]{2,1,0:T(8,128)} %state.1, bf16[1,128,512]{2,1,0:T(8,128)(2,1)} %tendency.1, bf16[1,128,512]{2,1,0:T(8,128)(2,1)} %diffusion.1, f32[1,128,128]{2,1,0:T(8,128)} %mixing.1, ...), custom_call_target="tpu_custom_call" | custom-call | flops 700000000 | bytes 1500000 | tf_op jit(solution)/shard_map/pallas_call | solution.py:628
  24.1 2.2 %shard_map.159 = (f32[1,128,512]{2,1,0:T(8,128)}, f32[2,16,256]{2,1,0:T(8,128)}) custom-call(f32[1,128,512]{2,1,0:T(8,128)} %get-tuple-element.6.state, f32[1,4,16,128]{3,2,1,0:T(8,128)} %get-tuple-element.7.parts, f32[4,8,8,128]{3,2,1,0:T(8,128)} %get-tuple-element.8.cols, f32[4,16,64]{2,1,0:T(8,128)} %get-tuple-element.9.weights, f32[128,256]{1,0:T(8,128)} %abel_matrix.1, ...), custom_call_target="tpu_custom_call" | custom-call | flops 10000000 | bytes 800000 | tf_op jit(solution)/shard_map/pallas_call | solution.py:644
